TPU v7x, 32 devices: a whole 2x2x4 slice. The times are simulated.
32 devices in a mesh: seq: 16 (over z, y, x), chan: 2 (over core).
Axes of the slice: x: 2, y: 2, z: 4, core: 2. Of those that a mesh axis runs over, the one named last changes fastest.
Arguments:
- hidden_in: bfloat16 [2048, 8192], P('seq', 'chan'), as said below
- query_mr: bfloat16 [2048, 8192], P('seq', 'chan'), may hold values from -6 to 6
- key_mr: bfloat16 [2048, 8192], P('seq', 'chan'), may hold values from -6 to 6
- value_mr: bfloat16 [2048, 8192], P('seq', 'chan'), may hold values from -6 to 6
- query_li: bfloat16 [2048, 8192], P('seq', 'chan'), may hold values from -6 to 6
- key_li: bfloat16 [2048, 8192], P('seq', 'chan'), may hold values from -6 to 6
- mr_filter: bfloat16 [128, 512], P(None, 'chan'), may hold values from -0.5 to 0.5
- li_rate: float32 [16, 8192], P(None, 'chan'), as said below
- li_residue: float32 [16, 8192], P(None, 'chan'), may hold values from -4 to 4
- norm_gain: float32 [8192], P('chan'), may hold values from 0.25 to 1.75
Outputs:
- normed_out: bfloat16 [2048, 8192], P('seq', 'chan')
Inputs may be any that keep to these rules, and one draw needn't show every extreme that they name: `hidden_in`: real values of moderate size. `li_rate`: decay rates per position, all positive, from 1 / 20480 to 1 / 30.
All inputs are finite; a program needn't handle non-finite values.
Results may differ from a plain program's by a relative error of at most 0.0055.
Values may be sent and summed in bfloat16 or wider, within the bound.
A program may use at most 128 MiB of HBM per device.

v0:
```python
import jax
import jax.numpy as jnp
from jax import lax
from jax.sharding import PartitionSpec as P


def passed_along(block, axis, distance):
    devices = range(lax.axis_size(axis))
    route = [(i - distance, i) for i in devices if i - distance in devices]
    return lax.ppermute(block, axis, route)


def band_matrix(filter_taps, filter_len):
    group_count = filter_taps.shape[1]
    padded = jnp.concatenate(
        [
            jnp.zeros((1, group_count), filter_taps.dtype),
            jnp.flip(filter_taps, 0),
            jnp.zeros((filter_len, group_count), filter_taps.dtype),
        ],
        0,
    )
    repeated = jnp.tile(padded, (filter_len, 1))[: filter_len * 2 * filter_len]
    return repeated.reshape(filter_len, 2 * filter_len, group_count)


def band_apply(toeplitz, earlier, latter, group_count):
    rows, channels = earlier.shape
    filter_len = toeplitz.shape[0]
    blocks = rows // filter_len
    earlier_rows = earlier.reshape(blocks, filter_len, group_count, channels // group_count)
    latter_rows = latter.reshape(blocks, filter_len, group_count, channels // group_count)
    windows = jnp.concatenate([earlier_rows, latter_rows], 1)
    result = jnp.einsum("tsg,bsgk->btgk", toeplitz, windows, preferred_element_type=jnp.float32)
    return result.reshape(rows, channels)


def per_device(
    hidden_in,
    query_mr,
    key_mr,
    value_mr,
    query_li,
    key_li,
    mr_filter,
    li_rate,
    li_residue,
    norm_gain,
):
    tokens, channels = key_mr.shape
    filter_len = mr_filter.shape[0]
    group_count = mr_filter.shape[1]
    highest = lax.Precision.HIGHEST
    product = (key_mr.astype(jnp.float32) * value_mr.astype(jnp.float32)).astype(jnp.bfloat16)
    toeplitz = band_matrix(mr_filter, filter_len)
    prior_rows = passed_along(product[tokens - filter_len + 1 :], "seq", 1)
    first_earlier = jnp.concatenate([jnp.zeros((1, channels), jnp.bfloat16), prior_rows], 0)
    earlier_all = jnp.concatenate([first_earlier, product[: tokens - filter_len]], 0)
    conv_mr = band_apply(toeplitz, earlier_all, product, group_count)
    out_mr = (query_mr.astype(jnp.float32) * conv_mr).astype(jnp.bfloat16)
    source = key_li.astype(jnp.float32) * out_mr.astype(jnp.float32)
    block_len = 16
    block_count = tokens // block_len
    scaled = li_residue * jnp.sqrt(-jnp.expm1(-2.0 * li_rate))
    lag_steps = jnp.arange(block_len).astype(jnp.float32)
    mode_taps = jnp.sum(scaled[None] * jnp.exp(-lag_steps[:, None, None] * li_rate[None]), 1)
    lag_index = jnp.arange(block_len)
    lag_grid = lag_index[:, None] - lag_index[None, :]
    selector = (lag_grid[:, :, None] == lag_index[None, None, :]).astype(jnp.float32)
    intra_block = jnp.einsum("tsd,dc->tsc", selector, mode_taps, precision=highest)
    decay_out = jnp.exp(-(block_len - 1 - lag_steps)[:, None, None] * li_rate[None])
    decay_in = scaled[None] * jnp.exp(-(lag_steps + 1.0)[:, None, None] * li_rate[None])
    blocks_in = source.reshape(block_count, block_len, channels)
    local_part = jnp.einsum("tsc,bsc->btc", intra_block, blocks_in, precision=highest)
    block_ends = jnp.einsum("snc,bsc->bnc", decay_out, blocks_in, precision=highest)
    block_decay = jnp.exp(-block_len * li_rate)

    def combine_blocks(earlier, latter):
        return (earlier[0] * latter[0], latter[0] * earlier[1] + latter[1])

    _, inclusive = lax.associative_scan(
        combine_blocks, (jnp.broadcast_to(block_decay[None], block_ends.shape), block_ends), axis=0
    )
    position = lax.axis_index("seq")
    shard_rows = lax.all_gather(inclusive[-1:], "seq", axis=0, tiled=True)
    owners = jnp.arange(shard_rows.shape[0], dtype=jnp.int32)
    distance = jnp.maximum(position - 1 - owners, 0).astype(jnp.float32)
    weight = jnp.where(
        (owners < position)[:, None, None],
        jnp.exp(-(tokens * distance)[:, None, None] * li_rate[None]),
        0.0,
    )
    incoming = jnp.sum(weight * shard_rows, 0)
    offsets = jnp.arange(block_count).astype(jnp.float32) * block_len
    start_states = (
        jnp.concatenate([jnp.zeros_like(inclusive[:1]), inclusive[:-1]], 0)
        + jnp.exp(-offsets[:, None, None] * li_rate[None]) * incoming[None]
    )
    from_states = jnp.einsum("tnc,bnc->btc", decay_in, start_states, precision=highest)
    conv_li = (local_part + from_states).reshape(tokens, channels)
    combined = (
        hidden_in.astype(jnp.float32)
        + out_mr.astype(jnp.float32)
        + query_li.astype(jnp.float32) * conv_li
    )
    local_squares = jnp.sum(combined * combined, axis=1)
    square_sum = lax.psum(local_squares, "chan")
    inverse_rms = lax.rsqrt(square_sum / (channels * lax.axis_size("chan")) + 1e-06)
    return (combined * inverse_rms[:, None] * norm_gain[None, :]).astype(jnp.bfloat16)


def solution(mesh):
    in_specs = (
        P("seq", "chan"),
        P("seq", "chan"),
        P("seq", "chan"),
        P("seq", "chan"),
        P("seq", "chan"),
        P("seq", "chan"),
        P(None, "chan"),
        P(None, "chan"),
        P(None, "chan"),
        P("chan"),
    )
    out_specs = P("seq", "chan")
    return jax.shard_map(
        per_device, mesh=mesh, in_specs=in_specs, out_specs=out_specs, check_vma=False
    )
```

profile of v0, /device:TPU:0, one launch (start us, length us, event | category | flops | bytes accessed | tf_op | source)
XLA Modules:
  0.0 453.9 jit_solution(3589061133464831685)
XLA Ops:
  6.5 0.0 all-gather.2.cloned.1.call-start
  6.5 1.8 multiply_convert_fusion.2
  8.4 0.3 slice.90
  8.6 4.9 %collective-permute-start = (bf16[127,4096]{1,0:T(8,128)(2,1)S(1)}, bf16[127,4096]{1,0:T(8,128)(2,1)S(1)}, u32[]{:S(2)}, u32[]{:S(2)}) collective-permute-start(bf16[127,4096]{1,0:T(8,128)(2,1)S(1)} %slice.90), channel_id=1, source_target_pairs={{0,2},{2,4},{4,6},{6,8},{8,10},{10,12},{12,14},{14,16},{16,18},{18... | collective-permute-start | bytes 3121160 | tf_op jit(solution)/shard_map/ppermute | solution.py:10
  13.6 0.0 copy-done.10
  13.6 0.7 rev.4
  14.3 0.1 pad.34.clone
  14.4 0.0 copy-done
  14.4 2.7 multiply_exponential_fusion
  17.0 0.0 copy-done.9
  17.0 0.1 maximum_maximum_fusion
  17.2 1.3 copy.105
  18.5 6.2 %tile.4 = bf16[128,257,256]{2,1,0:T(8,128)(2,1)} broadcast(bf16[257,256]{1,0:T(8,128)(2,1)S(1)} %maximum_maximum_fusion), dimensions={1,2} | broadcast | bytes 16974336 | tf_op jit(solution)/shard_map/tile | solution.py:23
  24.7 19.2 %tile.10 = bf16[32896,256]{1,0:T(8,128)(2,1)} reshape(bf16[128,257,256]{2,1,0:T(8,128)(2,1)} %tile.4) | data formatting | bytes 33685504 | tf_op jit(solution)/shard_map/tile | solution.py:23
  44.0 13.7 %slice.91 = bf16[32768,256]{1,0:T(8,128)(2,1)} slice(bf16[32896,256]{1,0:T(8,128)(2,1)} %tile.10), slice={[0:32768], [0:256]} | slice | bytes 33554432 | tf_op jit(solution)/shard_map/slice | solution.py:23
  57.7 23.5 %copy.119 = bf16[128,256,256]{1,0,2:T(8,128)(2,1)} copy(bf16[128,256,256]{2,1,0:T(8,128)(2,1)} %bitcast.41) | data formatting | bytes 33554432 | tf_op jit(solution)/shard_map/reshape | solution.py:24
  81.1 18.0 %copy.113 = f32[16,16,4096]{1,0,2:T(8,128)} copy(f32[16,16,4096]{2,1,0:T(8,128)} %multiply_exponential_fusion) | data formatting | bytes 8388608 | tf_op jit(solution)/shard_map/exp | solution.py:71
  99.2 0.0 copy-done.8
  99.2 1.0 sqrt_multiply_fusion
  100.1 0.0 collective-permute-done
  100.1 0.7 copy.122
  100.8 0.4 concatenate.18.clone
  101.2 10.6 %fusion.1 = f32[256,16,128]{2,1,0:T(8,128)S(1)} fusion(bf16[128,256,256]{1,0,2:T(8,128)(2,1)} %copy.119, bf16[1,128,256,16]{1,3,2,0:T(8,128)(2,1)} %bitcast.48, bf16[1,128,256,16]{1,3,2,0:T(8,128)(2,1)S(1)} %bitcast.47), kind=kOutput, calls=%fused_computation.9 | convolution fusion | flops 272629760 | bytes 20971520 | tf_op jit(solution)/shard_map/tsg,bsgk->btgk/dot_general | solution.py:34
  111.8 1.9 copy.107
  113.7 0.0 copy-done.5
  113.7 3.2 convert_multiply_fusion
  116.9 8.6 %copy.110 = f32[8,16,4096]{1,0,2:T(8,128)} copy(f32[8,16,4096]{2,1,0:T(8,128)S(1)} %bitcast.45) | data formatting | bytes 4194304 | tf_op jit(solution)/shard_map/reshape | solution.py:73
  125.5 34.4 %fusion.16 = f32[4096,8,16]{2,1,0:T(8,128)} fusion(f32[8,16,4096]{1,0,2:T(8,128)} %copy.110, f32[16,16,4096]{1,0,2:T(8,128)} %copy.113), kind=kOutput, calls=%fused_computation.53 | convolution fusion | flops 100663296 | bytes 8388608 | tf_op jit(solution)/shard_map/snc,bsc->bnc/dot_general | solution.py:75
  160.0 9.7 %copy.114 = f32[4096,8,16]{0,2,1:T(8,128)S(1)} copy(f32[4096,8,16]{2,1,0:T(8,128)} %fusion.16) | data formatting | bytes 4194304 | tf_op jit(solution)/shard_map/snc,bsc->bnc/dot_general | solution.py:75
  169.7 0.0 copy-done.4
  169.7 0.1 slice_add_fusion.1
  169.8 0.0 copy-done.7
  169.8 0.1 slice_add_fusion.2
  169.9 0.1 fusion.14
  170.0 0.1 fusion.13
  170.1 1.8 pad.23
  172.0 1.9 pad.24
  173.9 1.6 add.77
  175.5 2.8 pad.65
  178.3 1.7 slice.129
  180.0 0.0 all-gather.2.cloned.1.call-update
  180.1 2.9 pad.26
  183.0 1.6 fusion.4
  184.6 0.0 copy-start.2
  184.6 0.1 pad_maximum_fusion
  184.6 2.9 pad.25
  187.6 0.0 copy-done.2
  187.6 3.1 slice_add_fusion
  190.6 65.9 %all-gather.2.cloned.1.call-done = f32[16,16,4096]{2,1,0:T(8,128)} async-done(((f32[1,16,4096]{2,1,0:T(8,128)}), f32[16,16,4096]{2,1,0:T(8,128)}) %all-gather.2.cloned.1.call-update) | async-done | bytes 4194320 | tf_op jit(solution)/shard_map/all_gather | solution.py:85
  256.5 5.6 %multiply_reduce_fusion = (f32[16,4096]{1,0:T(8,128)S(1)}, f32[16,4096]{1,0:T(8,128)S(1)}, f32[16,16,4096]{2,1,0:T(8,128)}) fusion(f32[16,16,4096]{2,1,0:T(8,128)} %all-gather.2.cloned.1.call-done, f32[16]{0:T(128)S(1)} %get-tuple-element.18, f32[16,4096]{1,0:T(8,128)S(1)} %copy-done, pred[16]{0:T(512)(128)(4,1)S(1)} %iota_compare_fusion.2, ...), kind=kLoop, calls=%fused_computation.2 | loop fusion | flops 9306112 | bytes 9437392 | tf_op jit(solution)/shard_map/reduce_sum | solution.py:93
  262.1 3.9 fusion.8
  266.0 18.0 %copy.111 = f32[16,16,4096]{1,0,2:T(8,128)} copy(f32[16,16,4096]{2,1,0:T(8,128)} %fusion.8) | data formatting | bytes 8388608 | tf_op jit(solution)/shard_map/tsd,dc->tsc/dot_general | solution.py:70
  284.0 58.5 %fusion.15 = f32[4096,8,16]{2,1,0:T(8,128)} fusion(f32[8,16,4096]{1,0,2:T(8,128)} %copy.110, f32[16,16,4096]{1,0,2:T(8,128)} %copy.111), kind=kOutput, calls=%fused_computation.52 | convolution fusion | flops 100663296 | bytes 8388608 | tf_op jit(solution)/shard_map/tsc,bsc->btc/dot_general | solution.py:74
  342.5 0.0 copy-done.3
  342.5 0.4 multiply_add_fusion
  342.9 8.7 %copy.115 = f32[8,16,4096]{1,0,2:T(8,128)} copy(f32[8,16,4096]{2,1,0:T(8,128)S(1)} %multiply_add_fusion) | data formatting | bytes 4194304 | tf_op jit(solution)/shard_map/add | solution.py:96
  351.5 18.0 %copy.116 = f32[16,16,4096]{1,0,2:T(8,128)} copy(f32[16,16,4096]{2,1,0:T(8,128)} %get-tuple-element.11) | data formatting | bytes 8388608 | tf_op jit(solution)/shard_map/mul | solution.py:72
  369.5 59.3 %add_bitcast_fusion = f32[8,16,4096]{1,0,2:T(8,128)} fusion(f32[4096,8,16]{2,1,0:T(8,128)} %fusion.15, f32[8,16,4096]{1,0,2:T(8,128)} %copy.115, f32[16,16,4096]{1,0,2:T(8,128)} %copy.116), kind=kOutput, calls=%fused_computation | convolution fusion | flops 101187584 | bytes 10485760 | tf_op jit(solution)/shard_map/tnc,bnc->btc/dot_general | solution.py:99
  428.8 9.7 %copy.117 = f32[8,16,4096]{2,1,0:T(8,128)S(1)} copy(f32[8,16,4096]{1,0,2:T(8,128)} %add_bitcast_fusion) | data formatting | bytes 4194304 | tf_op jit(solution)/shard_map/add | solution.py:100
  438.5 0.0 copy-start.11
  438.5 2.3 multiply_reduce_fusion.2
  440.8 2.5 psum.7
  443.3 0.0 copy-done.11
  443.3 3.3 multiply_convert_fusion
  (24 shorter events, 0.2 us)
Async XLA Ops:
  6.5 7.0 %copy-start.10 = (bf16[128,256]{1,0:T(8,128)(2,1)S(1)}, bf16[128,256]{1,0:T(8,128)(2,1)}, u32[]{:S(2)}) copy-start(bf16[128,256]{1,0:T(8,128)(2,1)} %param.16) | copy-start | bytes 196612
  6.5 7.8 %copy-start = (f32[16,4096]{1,0:T(8,128)S(1)}, f32[16,4096]{1,0:T(8,128)}, u32[]{:S(2)}) copy-start(f32[16,4096]{1,0:T(8,128)} %param.17) | copy-start | bytes 786436
  6.5 250.0 %all-gather.2.cloned.1.call-start = ((), (), s32[]{:S(2)}) async-start(), calls=%async_computation | async-start | bytes 4456448 | tf_op jit(solution)/shard_map/all_gather | solution.py:85
  8.6 91.5 %collective-permute-start = (bf16[127,4096]{1,0:T(8,128)(2,1)S(1)}, bf16[127,4096]{1,0:T(8,128)(2,1)S(1)}, u32[]{:S(2)}, u32[]{:S(2)}) collective-permute-start(bf16[127,4096]{1,0:T(8,128)(2,1)S(1)} %slice.90), channel_id=1, source_target_pairs={{0,2},{2,4},{4,6},{6,8},{8,10},{10,12},{12,14},{14,16},{16,18},{18... | collective-permute-start | bytes 3121160 | tf_op jit(solution)/shard_map/ppermute | solution.py:10
  14.3 2.8 copy-start.9
  81.1 18.0 %copy-start.8 = (f32[16,4096]{1,0:T(8,128)S(1)}, f32[16,4096]{1,0:T(8,128)}, u32[]{:S(2)}) copy-start(f32[16,4096]{1,0:T(8,128)} %param.18) | copy-start | bytes 786436
  111.8 1.9 copy-start.5
  160.0 9.7 %copy-start.4 = (f32[16,4096]{1,0:T(8,128)S(1)}, f32[16,4096]{1,0:T(8,128)}, u32[]{:S(2)}) copy-start(f32[16,4096]{1,0:T(8,128)} %get-tuple-element.16) | copy-start | bytes 786436
  160.0 9.8 %copy-start.7 = (f32[16,4096]{1,0:T(8,128)S(1)}, f32[16,4096]{1,0:T(8,128)}, u32[]{:S(2)}) copy-start(f32[16,4096]{1,0:T(8,128)} %get-tuple-element.15) | copy-start | bytes 786436
  184.6 3.0 copy-start.2
  187.6 69.0 %copy-start.6 = (f32[16,4096]{1,0:T(8,128)S(1)}, f32[16,4096]{1,0:T(8,128)}, u32[]{:S(2)}) copy-start(f32[16,4096]{1,0:T(8,128)} %get-tuple-element.14) | copy-start | bytes 786436
  284.0 58.5 %copy-start.3 = (f32[7,16,4096]{2,1,0:T(8,128)S(1)}, f32[7,16,4096]{2,1,0:T(8,128)}, u32[]{:S(2)}) copy-start(f32[7,16,4096]{2,1,0:T(8,128)} %slice_add_fusion) | copy-start | bytes 5505028
  428.8 9.7 %copy-start.1 = (bf16[128,4096]{1,0:T(8,128)(2,1)S(1)}, bf16[128,4096]{1,0:T(8,128)(2,1)}, u32[]{:S(2)}) copy-start(bf16[128,4096]{1,0:T(8,128)(2,1)} %get-tuple-element.8) | copy-start | bytes 3145732
  438.5 4.8 %copy-start.11 = (f32[4096]{0:T(1024)S(1)}, f32[4096]{0:T(1024)}, u32[]{:S(2)}) copy-start(f32[4096]{0:T(1024)} %param.19) | copy-start | bytes 49156
Sparse Core Ops, SparseCore 0:
  180.2 76.3 all-gather.1
where the time goes:
time: 463 us; the launch traced here: 454 us
  local copies, waits for them, and re-layouts  173 us (37%)
  matrix products  167 us (36%)
  waiting for transfers between devices  65.9 us (14%)
  other arithmetic  27.2 us (6%)
  between operations  14.1 us (3%)
  starting transfers between devices  4.91 us (1%)
    all_gather x1, waiting for transfers between devices, per_device(): shard_rows = lax.all_gather(inclusive[-1:], 'seq', axis=0, tiled=True)  65.9 us
    dot_general x1, matrix products, per_device(): jnp.einsum('tnc,bnc->btc', decay_in, start_states, precision=highest)  59.3 us
    dot_general x1, matrix products, per_device(): jnp.einsum('tsc,bsc->btc', intra_block, blocks_in, precision=highest)  58.5 us
    dot_general x1, matrix products, per_device(): jnp.einsum('snc,bsc->bnc', decay_out, blocks_in, precision=highest)  34.4 us
    another operation x2, local copies, waits for them, and re-layouts, band_matrix(): repeated = jnp.tile(padded, (filter_len, 1))[:filter_len * 2 * filter_len]  25.5 us
    reshape x1, local copies, waits for them, and re-layouts, band_matrix(): return repeated.reshape(filter_len, 2 * filter_len, group_count)  23.5 us
    exp x1, local copies, waits for them, and re-layouts, per_device(): jnp.exp(-(block_len - 1 - lag_steps)[:, None, None] * li_rate[None])  18 us
    dot_general x1, local copies, waits for them, and re-layouts, per_device(): jnp.einsum('tsd,dc->tsc', selector, mode_taps, precision=highest)  18 us
  transfers between devices with their start and end apart: 2, of which 1 were waited for; matrix products, arithmetic and copies ran while one was open for 21% of the time, Pallas kernels for 0%

commit v1 on v0

v1 whole, which is shorter than its diff:
```python
import functools

import jax
import jax.numpy as jnp
from jax import lax
from jax.experimental import pallas as pl
from jax.experimental.pallas import tpu as pltpu
from jax.sharding import PartitionSpec as P

LANES = 128
SUBS = 8
CHUNK = LANES * SUBS
f32 = jnp.float32
bf16 = jnp.bfloat16


def mixer_kernel(
    seq_n, chan_n, chunks, group_width,
    hid_h, qmr_h, kmr_h, vmr_h, qli_h, kli_h, filt_h, rate_h, resid_h, gain_h,
    out_h,
    hid, qmr, kmr, vmr, qli, kli, filt, rate_in, resid_in, ngain,
    prod, halo, outb, taps, upper, acc, src, rate, mgain,
    prefix, total, state_out, state_in, squares_out, squares_in,
    in_sem, par_sem, out_sem, halo_send, halo_recv,
    st_send, st_recv, sq_send, sq_recv,
):
    pos = lax.axis_index("seq")
    lane_pos = lax.axis_index("chan")
    tokens = hid.shape[1]
    modes = rate_in.shape[0]
    slab = modes * SUBS
    rounds = seq_n.bit_length() - 1
    per_block = LANES // group_width
    nxt = lax.rem(pos + 1, seq_n)
    prv = lax.rem(pos + seq_n - 1, seq_n)

    def cols(k):
        return pl.ds(k * CHUNK, CHUNK)

    pairs = ((kmr_h, kmr), (vmr_h, vmr), (qmr_h, qmr), (kli_h, kli), (hid_h, hid), (qli_h, qli))

    def in_copy(a, k):
        return pltpu.make_async_copy(pairs[a][0].at[:, cols(k)], pairs[a][1].at[k], in_sem.at[a, k])

    par_copies = [
        pltpu.make_async_copy(h, v, par_sem.at[i])
        for i, (h, v) in enumerate(
            ((filt_h, filt), (rate_h, rate_in), (resid_h, resid_in), (gain_h, ngain))
        )
    ]
    for k in range(chunks):
        in_copy(0, k).start()
        in_copy(1, k).start()
    for c in par_copies:
        c.start()
    for a in range(2, 6):
        for k in range(chunks):
            in_copy(a, k).start()

    barrier = pltpu.get_barrier_semaphore()

    def greet(ids):
        pl.semaphore_signal(barrier, inc=1, device_id=ids, device_id_type=pl.DeviceIdType.MESH)

    greet({"seq": nxt})
    greet({"seq": prv})
    bits = [lax.rem(pos // (1 << r), 2) for r in range(rounds)]
    partners = [pos + (1 << r) * (1 - 2 * bits[r]) for r in range(rounds)]
    for r in range(rounds):
        greet({"seq": partners[r]})
    for d in range(1, chan_n):
        greet({"chan": lax.rem(lane_pos + d, chan_n)})

    def halo_copy(k):
        return pltpu.make_async_remote_copy(
            src_ref=prod.at[k], dst_ref=halo.at[k],
            send_sem=halo_send.at[k], recv_sem=halo_recv.at[k],
            device_id={"seq": nxt}, device_id_type=pl.DeviceIdType.MESH,
        )

    def state_copy(r, k):
        return pltpu.make_async_remote_copy(
            src_ref=state_out.at[r, k], dst_ref=state_in.at[r, k],
            send_sem=st_send.at[r, k], recv_sem=st_recv.at[r, k],
            device_id={"seq": partners[r]}, device_id_type=pl.DeviceIdType.MESH,
        )

    def squares_copy(d):
        return pltpu.make_async_remote_copy(
            src_ref=squares_out, dst_ref=squares_in.at[d - 1],
            send_sem=sq_send.at[d - 1], recv_sem=sq_recv.at[d - 1],
            device_id={"chan": lax.rem(lane_pos + d, chan_n)},
            device_id_type=pl.DeviceIdType.MESH,
        )

    @pl.when(pos == 0)
    def _():
        halo[...] = jnp.zeros_like(halo)

    for k in range(chunks):
        in_copy(0, k).wait()
        in_copy(1, k).wait()
        prod[k] = (kmr[k].astype(f32) * vmr[k].astype(f32)).astype(bf16)
        if k == 0:
            pl.semaphore_wait(barrier, 2 + rounds + chan_n - 1)

        @pl.when(pos < seq_n - 1)
        def _():
            halo_copy(k).start()

    for c in par_copies:
        c.wait()

    tap_i = lax.broadcasted_iota(jnp.int32, (tokens, tokens), 0)
    pos_i = lax.broadcasted_iota(jnp.int32, (tokens, tokens), 1)
    wrap = jnp.where(lax.rem(tap_i + pos_i, tokens) == 0, 1.0, 0.0).astype(bf16)
    taps[...] = lax.dot_general(
        filt[...], wrap, (((0,), (0,)), ((), ())), preferred_element_type=f32
    )

    for k in range(chunks):
        for b in range(SUBS):
            lanes = pl.ds(k * CHUNK + b * LANES, LANES)
            r = rate_in[:, lanes]
            x = 2.0 * r
            series = x * (
                1.0 - x * (1 / 2) * (1.0 - x * (1 / 3) * (1.0 - x * (1 / 4) * (
                    1.0 - x * (1 / 5) * (1.0 - x * (1 / 6) * (1.0 - x * (1 / 7))))))
            )
            grown = jnp.where(x < 0.1, series, 1.0 - jnp.exp(-x))
            rows = pl.ds(k * slab + b, modes, stride=SUBS)
            rate[rows, :] = r
            mgain[rows, :] = resid_in[:, lanes] * jnp.sqrt(grown)

    def spread(x):
        lane = lax.broadcasted_iota(jnp.int32, x.shape, 1)
        wide = x.astype(f32)
        return jnp.concatenate(
            [
                jnp.where(lane // group_width == g, wide, 0.0).astype(bf16)
                for g in range(per_block)
            ],
            0,
        )

    row_i = lax.broadcasted_iota(jnp.int32, (tokens, LANES), 0)
    lane_i = lax.broadcasted_iota(jnp.int32, (tokens, LANES), 1)
    lower_mask = lane_i <= row_i

    for k in range(chunks):

        def local_block(b, carry):
            j = k * SUBS + b
            lanes = pl.ds(pl.multiple_of(b * LANES, LANES), LANES)
            rows = taps[pl.ds(pl.multiple_of(j * per_block, per_block), per_block), :]
            lows, ups = [], []
            for g in range(per_block):
                ring = pltpu.roll(
                    jnp.broadcast_to(rows[g : g + 1, :], (tokens, LANES)),
                    0, 1, stride=1, stride_axis=0,
                )
                lows.append(jnp.where(lower_mask, ring, 0.0).astype(bf16))
                ups.append(jnp.where(lower_mask, 0.0, ring).astype(bf16))
            upper[j] = jnp.concatenate(ups, 1)
            acc[k, :, lanes] = jnp.dot(
                jnp.concatenate(lows, 1), spread(prod[k, :, lanes]), preferred_element_type=f32
            )
            return carry

        lax.fori_loop(0, SUBS, local_block, 0)

    def chunk_rate(k):
        return rate[pl.ds(k * slab, slab), :]

    def chunk_mode(ref, k, n):
        return ref[pl.ds(k * slab + n * SUBS, SUBS), :]

    def medium_and_states(k):
        @pl.when(pos > 0)
        def _():
            halo_copy(k).wait_recv()

        for a in range(2, 5):
            in_copy(a, k).wait()

        def block(b, carry):
            j = k * SUBS + b
            lanes = pl.ds(pl.multiple_of(b * LANES, LANES), LANES)
            conv = acc[k, :, lanes] + jnp.dot(
                upper[j], spread(halo[k, :, lanes]), preferred_element_type=f32
            )
            out_mr = (qmr[k, :, lanes].astype(f32) * conv).astype(bf16).astype(f32)
            src[pl.ds(pl.multiple_of(j * tokens, tokens), tokens), :] = (
                kli[k, :, lanes].astype(f32) * out_mr
            )
            acc[k, :, lanes] = hid[k, :, lanes].astype(f32) + out_mr
            return carry

        lax.fori_loop(0, SUBS, block, 0)

        decay = [jnp.exp(-chunk_mode(rate, k, n)) for n in range(modes)]
        gain = [chunk_mode(mgain, k, n) for n in range(modes)]

        def step(t, states):
            at = pl.ds(k * SUBS * tokens + t, SUBS, stride=tokens)
            x = src[at, :]
            states = tuple(decay[n] * states[n] + x for n in range(modes))
            parts = [gain[n] * states[n] for n in range(modes)]
            while len(parts) > 1:
                parts = [a + b for a, b in zip(parts[::2], parts[1::2])]
            src[at, :] = parts[0]
            return states

        zero = jnp.zeros((SUBS, LANES), f32)
        states = lax.fori_loop(0, tokens, step, (zero,) * modes, unroll=4)
        for n in range(modes):
            total[k, pl.ds(n * SUBS, SUBS), :] = states[n]
        prefix[k] = jnp.zeros((slab, LANES), f32)

    def send_state(r, k):
        def go():
            state_out[r, k] = total[k].astype(bf16)
            state_copy(r, k).start()

        if r < rounds - 1:
            go()
        else:
            pl.when(bits[r] == 0)(go)

    def take_state(r, k):
        span = 1 << r
        if r < rounds - 1:
            state_copy(r, k).wait_recv()
            got = state_in[r, k].astype(f32)
            rates = chunk_rate(k)
            whole = jnp.exp(rates * (-1.0 * tokens * span))
            upper_half = bits[r] == 1
            ahead = (tokens * lax.rem(pos, span)).astype(f32)
            weight = jnp.exp(-rates * ahead)
            mine = total[k]
            prefix[k] = prefix[k] + jnp.where(upper_half, weight * got, 0.0)
            total[k] = jnp.where(upper_half, whole * got + mine, whole * mine + got)
        else:

            @pl.when(bits[r] == 1)
            def _():
                state_copy(r, k).wait_recv()
                got = state_in[r, k].astype(f32)
                ahead = (tokens * lax.rem(pos, span)).astype(f32)
                prefix[k] = prefix[k] + jnp.exp(-chunk_rate(k) * ahead) * got

    def finish_chunk(k):
        decay = [jnp.exp(-chunk_mode(rate, k, n)) for n in range(modes)]
        start = tuple(
            chunk_mode(mgain, k, n) * prefix[k, pl.ds(n * SUBS, SUBS), :] for n in range(modes)
        )

        def step(t, waves):
            at = pl.ds(k * SUBS * tokens + t, SUBS, stride=tokens)
            waves = tuple(decay[n] * waves[n] for n in range(modes))
            parts = list(waves)
            while len(parts) > 1:
                parts = [a + b for a, b in zip(parts[::2], parts[1::2])]
            src[at, :] = src[at, :] + parts[0]
            return waves

        lax.fori_loop(0, tokens, step, start, unroll=4)
        in_copy(5, k).wait()

        def block(b, carry):
            j = k * SUBS + b
            lanes = pl.ds(pl.multiple_of(b * LANES, LANES), LANES)
            conv = src[pl.ds(pl.multiple_of(j * tokens, tokens), tokens), :]
            combined = acc[k, :, lanes] + qli[k, :, lanes].astype(f32) * conv
            acc[k, :, lanes] = combined
            squares_out[...] += combined * combined
            return carry

        lax.fori_loop(0, SUBS, block, 0)

    squares_out[...] = jnp.zeros_like(squares_out)
    for turn in range(chunks + rounds):
        for k in range(chunks):
            r = turn - k - 1
            if 0 <= r < rounds:
                take_state(r, k)
                if r + 1 < rounds:
                    send_state(r + 1, k)
        if turn < chunks:
            medium_and_states(turn)
            send_state(0, turn)
        done = turn - rounds
        if 0 <= done < chunks:
            finish_chunk(done)

    sums = squares_out[...]
    for d in range(1, chan_n):
        squares_copy(d).start()
    for d in range(1, chan_n):
        squares_copy(d).wait_recv()
        sums = sums + squares_in[d - 1]
    width = chunks * CHUNK * chan_n
    inverse = lax.rsqrt(jnp.sum(sums, 1, keepdims=True) / width + 1e-06)

    for k in range(chunks):
        outb[k] = (acc[k] * inverse * ngain[:, cols(k)]).astype(bf16)
        pltpu.make_async_copy(outb.at[k], out_h.at[:, cols(k)], out_sem.at[k]).start()

    for k in range(chunks):
        pltpu.make_async_copy(outb.at[k], out_h.at[:, cols(k)], out_sem.at[k]).wait()

        @pl.when(pos < seq_n - 1)
        def _():
            halo_copy(k).wait_send()

        for r in range(rounds - 1):
            state_copy(r, k).wait_send()

        @pl.when(bits[rounds - 1] == 0)
        def _():
            state_copy(rounds - 1, k).wait_send()

    for d in range(1, chan_n):
        squares_copy(d).wait_send()


def per_device(
    seq_n, chan_n,
    hidden_in, query_mr, key_mr, value_mr, query_li, key_li,
    mr_filter, li_rate, li_residue, norm_gain,
):
    tokens, channels = hidden_in.shape
    groups = mr_filter.shape[1]
    modes = li_rate.shape[0]
    chunks = channels // CHUNK
    rounds = seq_n.bit_length() - 1
    slab = modes * SUBS
    assert seq_n == 1 << rounds and tokens == mr_filter.shape[0] == LANES
    big = pltpu.VMEM((chunks, tokens, CHUNK), bf16)
    dma = pltpu.SemaphoreType.DMA
    return pl.pallas_call(
        functools.partial(mixer_kernel, seq_n, chan_n, chunks, channels // groups),
        out_shape=jax.ShapeDtypeStruct((tokens, channels), bf16),
        in_specs=[pl.BlockSpec(memory_space=pl.ANY)] * 10,
        out_specs=pl.BlockSpec(memory_space=pl.ANY),
        scratch_shapes=[
            big, big, big, big, big, big,
            pltpu.VMEM(mr_filter.shape, bf16),
            pltpu.VMEM(li_rate.shape, f32),
            pltpu.VMEM(li_residue.shape, f32),
            pltpu.VMEM((1, channels), f32),
            big, big, big,
            pltpu.VMEM((groups, tokens), f32),
            pltpu.VMEM((channels // LANES, tokens, tokens * LANES * groups // channels), bf16),
            pltpu.VMEM((chunks, tokens, CHUNK), f32),
            pltpu.VMEM((channels // LANES * tokens, LANES), f32),
            pltpu.VMEM((chunks * slab, LANES), f32),
            pltpu.VMEM((chunks * slab, LANES), f32),
            pltpu.VMEM((chunks, slab, LANES), f32),
            pltpu.VMEM((chunks, slab, LANES), f32),
            pltpu.VMEM((rounds, chunks, slab, LANES), bf16),
            pltpu.VMEM((rounds, chunks, slab, LANES), bf16),
            pltpu.VMEM((tokens, LANES), f32),
            pltpu.VMEM((max(chan_n - 1, 1), tokens, LANES), f32),
            dma((6, chunks)),
            dma((4,)),
            dma((chunks,)),
            dma((chunks,)),
            dma((chunks,)),
            dma((rounds, chunks)),
            dma((rounds, chunks)),
            dma((max(chan_n - 1, 1),)),
            dma((max(chan_n - 1, 1),)),
        ],
        compiler_params=pltpu.CompilerParams(
            collective_id=0, has_side_effects=True, vmem_limit_bytes=48 * 1024 * 1024
        ),
        cost_estimate=pl.CostEstimate(
            flops=4 * tokens * tokens * channels * LANES * groups // channels,
            bytes_accessed=14 * tokens * channels,
            transcendentals=4 * modes * channels,
        ),
        name="hyena_mixers",
    )(
        hidden_in, query_mr, key_mr, value_mr, query_li, key_li,
        mr_filter, li_rate, li_residue, norm_gain.reshape(1, channels),
    )


def solution(mesh):
    seq_n, chan_n = mesh.shape["seq"], mesh.shape["chan"]
    rows = P("seq", "chan")
    by_channel = P(None, "chan")
    in_specs = (rows,) * 6 + (by_channel,) * 3 + (P("chan"),)
    return jax.shard_map(
        functools.partial(per_device, seq_n, chan_n),
        mesh=mesh, in_specs=in_specs, out_specs=rows, check_vma=False,
    )
```

time: 463 us -> 70.4 us (0.15)
  the two profiles are of different devices: /device:TPU:0 before, /device:TPU:25 now
where the time goes in v1:
time: 70.4 us; the launch traced here: 69.4 us
  Pallas kernels  60.1 us (85%)
  local copies, waits for them, and re-layouts  9.32 us (13%)
    pallas_call x1, Pallas kernels, per_device(): pl.pallas_call(functools.partial(mixer_kernel, seq_n, chan_n, chunks, cha...  60.1 us
    unnamed x17, local copies, waits for them, and re-layouts  9.32 us

profile of v1, /device:TPU:25, one launch (start us, length us, event | category | flops | bytes accessed | tf_op | source)
XLA Modules:
  0.0 69.4 jit_solution(6602605221015123764)
XLA Ops:
  0.0 0.0 copy-start
  0.0 1.2 %copy-done = bf16[128,4096]{1,0:T(8,128)(2,1)S(1)} copy-done((bf16[128,4096]{1,0:T(8,128)(2,1)S(1)}, bf16[128,4096]{1,0:T(8,128)(2,1)}, u32[]{:S(2)}) %copy-start) | copy-done | bytes 1048600
  1.2 0.0 copy-start.1
  1.2 1.2 %copy-done.1 = bf16[128,4096]{1,0:T(8,128)(2,1)S(1)} copy-done((bf16[128,4096]{1,0:T(8,128)(2,1)S(1)}, bf16[128,4096]{1,0:T(8,128)(2,1)}, u32[]{:S(2)}) %copy-start.1) | copy-done | bytes 1048600
  2.5 0.0 copy-start.2
  2.5 1.2 %copy-done.2 = bf16[128,4096]{1,0:T(8,128)(2,1)S(1)} copy-done((bf16[128,4096]{1,0:T(8,128)(2,1)S(1)}, bf16[128,4096]{1,0:T(8,128)(2,1)}, u32[]{:S(2)}) %copy-start.2) | copy-done | bytes 1048600
  3.7 0.0 copy-start.3
  3.7 1.2 %copy-done.3 = bf16[128,4096]{1,0:T(8,128)(2,1)S(1)} copy-done((bf16[128,4096]{1,0:T(8,128)(2,1)S(1)}, bf16[128,4096]{1,0:T(8,128)(2,1)}, u32[]{:S(2)}) %copy-start.3) | copy-done | bytes 1048600
  4.9 0.0 copy-start.4
  4.9 0.9 %copy-done.4 = f32[16,4096]{1,0:T(8,128)S(1)} copy-done((f32[16,4096]{1,0:T(8,128)S(1)}, f32[16,4096]{1,0:T(8,128)}, u32[]{:S(2)}) %copy-start.4) | copy-done | bytes 262168
  5.9 0.0 copy-start.5
  5.9 0.9 %copy-done.5 = f32[16,4096]{1,0:T(8,128)S(1)} copy-done((f32[16,4096]{1,0:T(8,128)S(1)}, f32[16,4096]{1,0:T(8,128)}, u32[]{:S(2)}) %copy-start.5) | copy-done | bytes 262168
  6.8 0.0 copy-start.6
  6.8 0.8 %copy-done.6 = bf16[128,256]{1,0:T(8,128)(2,1)S(1)} copy-done((bf16[128,256]{1,0:T(8,128)(2,1)S(1)}, bf16[128,256]{1,0:T(8,128)(2,1)}, u32[]{:S(2)}) %copy-start.6) | copy-done | bytes 65560
  7.6 0.0 copy-start.7
  7.6 0.7 %copy-done.7 = f32[4096]{0:T(1024)S(1)} copy-done((f32[4096]{0:T(1024)S(1)}, f32[4096]{0:T(1024)}, u32[]{:S(2)}) %copy-start.7) | copy-done | bytes 16408
  8.4 60.1 %hyena_mixers.1 = bf16[128,4096]{1,0:T(8,128)(2,1)S(1)} custom-call(bf16[128,4096]{1,0:T(8,128)(2,1)S(1)} %copy-done, bf16[128,4096]{1,0:T(8,128)(2,1)S(1)} %copy-done.1, bf16[128,4096]{1,0:T(8,128)(2,1)S(1)} %copy-done.2, bf16[128,4096]{1,0:T(8,128)(2,1)S(1)} %copy-done.3, bf16[128,4096]{1,0:T(8,128)(2,1)} %qli_h.1, bf16[128,4096]{1,0:T(8,128)(2,1)} %kli_h.1, ...), custom_call_target="tpu_custom_call" | custom-call | flops 2147483648 | bytes 7340032 | tf_op jit(solution)/shard_map/hyena_mixers/pallas_call | solution.py:341
  68.5 1.0 %copy.12 = bf16[128,4096]{1,0:T(8,128)(2,1)} copy(bf16[128,4096]{1,0:T(8,128)(2,1)S(1)} %hyena_mixers.1) | data formatting | bytes 2097152
Async XLA Ops:
  0.0 1.2 %copy-start = (bf16[128,4096]{1,0:T(8,128)(2,1)S(1)}, bf16[128,4096]{1,0:T(8,128)(2,1)}, u32[]{:S(2)}) copy-start(bf16[128,4096]{1,0:T(8,128)(2,1)} %hid_h.1) | copy-start | bytes 3145732
  1.2 1.2 %copy-start.1 = (bf16[128,4096]{1,0:T(8,128)(2,1)S(1)}, bf16[128,4096]{1,0:T(8,128)(2,1)}, u32[]{:S(2)}) copy-start(bf16[128,4096]{1,0:T(8,128)(2,1)} %qmr_h.1) | copy-start | bytes 3145732
  2.5 1.2 %copy-start.2 = (bf16[128,4096]{1,0:T(8,128)(2,1)S(1)}, bf16[128,4096]{1,0:T(8,128)(2,1)}, u32[]{:S(2)}) copy-start(bf16[128,4096]{1,0:T(8,128)(2,1)} %kmr_h.1) | copy-start | bytes 3145732
  3.7 1.2 %copy-start.3 = (bf16[128,4096]{1,0:T(8,128)(2,1)S(1)}, bf16[128,4096]{1,0:T(8,128)(2,1)}, u32[]{:S(2)}) copy-start(bf16[128,4096]{1,0:T(8,128)(2,1)} %vmr_h.1) | copy-start | bytes 3145732
  4.9 0.9 %copy-start.4 = (f32[16,4096]{1,0:T(8,128)S(1)}, f32[16,4096]{1,0:T(8,128)}, u32[]{:S(2)}) copy-start(f32[16,4096]{1,0:T(8,128)} %rate_h.1) | copy-start | bytes 786436
  5.9 0.9 %copy-start.5 = (f32[16,4096]{1,0:T(8,128)S(1)}, f32[16,4096]{1,0:T(8,128)}, u32[]{:S(2)}) copy-start(f32[16,4096]{1,0:T(8,128)} %resid_h.1) | copy-start | bytes 786436
  6.8 0.8 %copy-start.6 = (bf16[128,256]{1,0:T(8,128)(2,1)S(1)}, bf16[128,256]{1,0:T(8,128)(2,1)}, u32[]{:S(2)}) copy-start(bf16[128,256]{1,0:T(8,128)(2,1)} %filt_h.1) | copy-start | bytes 196612
  7.6 0.7 %copy-start.7 = (f32[4096]{0:T(1024)S(1)}, f32[4096]{0:T(1024)}, u32[]{:S(2)}) copy-start(f32[4096]{0:T(1024)} %param.19) | copy-start | bytes 49156

commit v2 on v1

--- a/solution.py
+++ b/solution.py
@@ -212,7 +212,7 @@
             return states
 
         zero = jnp.zeros((SUBS, LANES), f32)
-        states = lax.fori_loop(0, tokens, step, (zero,) * modes, unroll=4)
+        states = lax.fori_loop(0, tokens, step, (zero,) * modes, unroll=16)
         for n in range(modes):
             total[k, pl.ds(n * SUBS, SUBS), :] = states[n]
         prefix[k] = jnp.zeros((slab, LANES), f32)
@@ -264,7 +264,7 @@
             src[at, :] = src[at, :] + parts[0]
             return waves
 
-        lax.fori_loop(0, tokens, step, start, unroll=4)
+        lax.fori_loop(0, tokens, step, start, unroll=16)
         in_copy(5, k).wait()
 
         def block(b, carry):
@@ -280,15 +280,15 @@
 
     squares_out[...] = jnp.zeros_like(squares_out)
     for turn in range(chunks + rounds):
+        if turn < chunks:
+            medium_and_states(turn)
+            send_state(0, turn)
         for k in range(chunks):
             r = turn - k - 1
             if 0 <= r < rounds:
                 take_state(r, k)
                 if r + 1 < rounds:
                     send_state(r + 1, k)
-        if turn < chunks:
-            medium_and_states(turn)
-            send_state(0, turn)
         done = turn - rounds
         if 0 <= done < chunks:
             finish_chunk(done)
@@ -373,7 +373,7 @@
             dma((max(chan_n - 1, 1),)),
         ],
         compiler_params=pltpu.CompilerParams(
-            collective_id=0, has_side_effects=True, vmem_limit_bytes=48 * 1024 * 1024
+            collective_id=0, has_side_effects=True, vmem_limit_bytes=63 * 1024 * 1024
         ),
         cost_estimate=pl.CostEstimate(
             flops=4 * tokens * tokens * channels * LANES * groups // channels,

time: 70.4 us -> 55.3 us (0.79)
  the two profiles are of different devices: /device:TPU:25 before, /device:TPU:19 now
where the time goes in v2:
time: 55.3 us; the launch traced here: 55.2 us
  Pallas kernels  52.9 us (96%)
  local copies, waits for them, and re-layouts  2.29 us (4%)
    pallas_call x1, Pallas kernels, per_device(): pl.pallas_call(functools.partial(mixer_kernel, seq_n, chan_n, chunks, cha...  52.9 us
    unnamed x1, local copies, waits for them, and re-layouts  2.29 us

profile of v2, /device:TPU:19, one launch (start us, length us, event | category | flops | bytes accessed | tf_op | source)
XLA Modules:
  0.0 55.2 jit_solution(2755747788614884017)
XLA Ops:
  0.0 52.9 %hyena_mixers.1 = bf16[128,4096]{1,0:T(8,128)(2,1)} custom-call(bf16[128,4096]{1,0:T(8,128)(2,1)} %hid_h.1, bf16[128,4096]{1,0:T(8,128)(2,1)} %qmr_h.1, bf16[128,4096]{1,0:T(8,128)(2,1)} %kmr_h.1, bf16[128,4096]{1,0:T(8,128)(2,1)} %vmr_h.1, bf16[128,4096]{1,0:T(8,128)(2,1)} %qli_h.1, bf16[128,4096]{1,0:T(8,128)(2,1)} %kli_h.1, bf16[128,256]{1,0:T(8,128)(2,1)} %filt_h.1, ...), custom_call_target="tpu_custom_call" | custom-call | flops 2147483648 | bytes 7340032 | tf_op jit(solution)/shard_map/hyena_mixers/pallas_call | solution.py:341
  52.9 2.3 %copy.12 = bf16[128,4096]{1,0:T(8,128)(2,1)} copy(bf16[128,4096]{1,0:T(8,128)(2,1)} %hyena_mixers.1) | data formatting | bytes 2097152

commit v3 on v2

--- a/solution.py
+++ b/solution.py
@@ -12,6 +12,16 @@
 CHUNK = LANES * SUBS
 f32 = jnp.float32
 bf16 = jnp.bfloat16
+
+
+def stages(seq_n):
+    radices, spans = [], []
+    span = 1
+    while span < seq_n:
+        radices.append(min(4, seq_n // span))
+        spans.append(span)
+        span *= radices[-1]
+    return radices, spans
 
 
 def mixer_kernel(
@@ -29,7 +39,8 @@
     tokens = hid.shape[1]
     modes = rate_in.shape[0]
     slab = modes * SUBS
-    rounds = seq_n.bit_length() - 1
+    radices, spans = stages(seq_n)
+    rounds = len(radices)
     per_block = LANES // group_width
     nxt = lax.rem(pos + 1, seq_n)
     prv = lax.rem(pos + seq_n - 1, seq_n)
@@ -64,10 +75,14 @@
 
     greet({"seq": nxt})
     greet({"seq": prv})
-    bits = [lax.rem(pos // (1 << r), 2) for r in range(rounds)]
-    partners = [pos + (1 << r) * (1 - 2 * bits[r]) for r in range(rounds)]
+    digits = [lax.rem(pos // m, q) for m, q in zip(spans, radices)]
+
+    def member(r, e):
+        return pos + spans[r] * (lax.rem(digits[r] + e, radices[r]) - digits[r])
+
     for r in range(rounds):
-        greet({"seq": partners[r]})
+        for e in range(1, radices[r]):
+            greet({"seq": member(r, e)})
     for d in range(1, chan_n):
         greet({"chan": lax.rem(lane_pos + d, chan_n)})
 
@@ -78,11 +93,11 @@
             device_id={"seq": nxt}, device_id_type=pl.DeviceIdType.MESH,
         )
 
-    def state_copy(r, k):
+    def state_copy(r, e, k):
         return pltpu.make_async_remote_copy(
-            src_ref=state_out.at[r, k], dst_ref=state_in.at[r, k],
-            send_sem=st_send.at[r, k], recv_sem=st_recv.at[r, k],
-            device_id={"seq": partners[r]}, device_id_type=pl.DeviceIdType.MESH,
+            src_ref=state_out.at[r, k], dst_ref=state_in.at[r, e - 1, k],
+            send_sem=st_send.at[r, e - 1, k], recv_sem=st_recv.at[r, e - 1, k],
+            device_id={"seq": member(r, e)}, device_id_type=pl.DeviceIdType.MESH,
         )
 
     def squares_copy(d):
@@ -102,7 +117,7 @@
         in_copy(1, k).wait()
         prod[k] = (kmr[k].astype(f32) * vmr[k].astype(f32)).astype(bf16)
         if k == 0:
-            pl.semaphore_wait(barrier, 2 + rounds + chan_n - 1)
+            pl.semaphore_wait(barrier, 2 + sum(radices) - rounds + chan_n - 1)
 
         @pl.when(pos < seq_n - 1)
         def _():
@@ -217,37 +232,46 @@
             total[k, pl.ds(n * SUBS, SUBS), :] = states[n]
         prefix[k] = jnp.zeros((slab, LANES), f32)
 
+    def sends(r, e, act):
+        if r < rounds - 1:
+            act()
+        else:
+            pl.when(digits[r] + e < radices[r])(act)
+
+    def takes(r, e, act):
+        if r < rounds - 1:
+            act()
+        else:
+            pl.when(digits[r] >= e)(act)
+
     def send_state(r, k):
-        def go():
-            state_out[r, k] = total[k].astype(bf16)
-            state_copy(r, k).start()
+        state_out[r, k] = total[k].astype(bf16)
+        for e in range(1, radices[r]):
+            sends(r, e, lambda: state_copy(r, e, k).start())
+
+    def take_state(r, k):
+        rates = chunk_rate(k)
+        span, radix, digit = spans[r], radices[r], digits[r]
+        inside = lax.rem(pos, span)
+
+        def faded(steps, x):
+            return jnp.exp(-rates * (tokens * steps).astype(f32)) * x
 
         if r < rounds - 1:
-            go()
-        else:
-            pl.when(bits[r] == 0)(go)
-
-    def take_state(r, k):
-        span = 1 << r
-        if r < rounds - 1:
-            state_copy(r, k).wait_recv()
-            got = state_in[r, k].astype(f32)
-            rates = chunk_rate(k)
-            whole = jnp.exp(rates * (-1.0 * tokens * span))
-            upper_half = bits[r] == 1
-            ahead = (tokens * lax.rem(pos, span)).astype(f32)
-            weight = jnp.exp(-rates * ahead)
-            mine = total[k]
-            prefix[k] = prefix[k] + jnp.where(upper_half, weight * got, 0.0)
-            total[k] = jnp.where(upper_half, whole * got + mine, whole * mine + got)
-        else:
-
-            @pl.when(bits[r] == 1)
-            def _():
-                state_copy(r, k).wait_recv()
-                got = state_in[r, k].astype(f32)
-                ahead = (tokens * lax.rem(pos, span)).astype(f32)
-                prefix[k] = prefix[k] + jnp.exp(-chunk_rate(k) * ahead) * got
+            total[k] = faded(span * (radix - 1 - digit), total[k])
+        for e in range(1, radix):
+
+            def take():
+                state_copy(r, e, k).wait_recv()
+                got = state_in[r, e - 1, k].astype(f32)
+                sender = lax.rem(digit + radix - e, radix)
+                earlier = sender < digit
+                ahead = jnp.where(earlier, span * (digit - 1 - sender) + inside, 0)
+                prefix[k] = prefix[k] + jnp.where(earlier, faded(ahead, got), 0.0)
+                if r < rounds - 1:
+                    total[k] = total[k] + faded(span * (radix - 1 - sender), got)
+
+            takes(r, e, take)
 
     def finish_chunk(k):
         decay = [jnp.exp(-chunk_mode(rate, k, n)) for n in range(modes)]
@@ -313,12 +337,9 @@
         def _():
             halo_copy(k).wait_send()
 
-        for r in range(rounds - 1):
-            state_copy(r, k).wait_send()
-
-        @pl.when(bits[rounds - 1] == 0)
-        def _():
-            state_copy(rounds - 1, k).wait_send()
+        for r in range(rounds):
+            for e in range(1, radices[r]):
+                sends(r, e, lambda: state_copy(r, e, k).wait_send())
 
     for d in range(1, chan_n):
         squares_copy(d).wait_send()
@@ -333,9 +354,10 @@
     groups = mr_filter.shape[1]
     modes = li_rate.shape[0]
     chunks = channels // CHUNK
-    rounds = seq_n.bit_length() - 1
+    radices, _ = stages(seq_n)
+    rounds, most = len(radices), max(radices) - 1
     slab = modes * SUBS
-    assert seq_n == 1 << rounds and tokens == mr_filter.shape[0] == LANES
+    assert seq_n & (seq_n - 1) == 0 and tokens == mr_filter.shape[0] == LANES
     big = pltpu.VMEM((chunks, tokens, CHUNK), bf16)
     dma = pltpu.SemaphoreType.DMA
     return pl.pallas_call(
@@ -359,7 +381,7 @@
             pltpu.VMEM((chunks, slab, LANES), f32),
             pltpu.VMEM((chunks, slab, LANES), f32),
             pltpu.VMEM((rounds, chunks, slab, LANES), bf16),
-            pltpu.VMEM((rounds, chunks, slab, LANES), bf16),
+            pltpu.VMEM((rounds, most, chunks, slab, LANES), bf16),
             pltpu.VMEM((tokens, LANES), f32),
             pltpu.VMEM((max(chan_n - 1, 1), tokens, LANES), f32),
             dma((6, chunks)),
@@ -367,8 +389,8 @@
             dma((chunks,)),
             dma((chunks,)),
             dma((chunks,)),
-            dma((rounds, chunks)),
-            dma((rounds, chunks)),
+            dma((rounds, most, chunks)),
+            dma((rounds, most, chunks)),
             dma((max(chan_n - 1, 1),)),
             dma((max(chan_n - 1, 1),)),
         ],

time: 55.3 us -> 53 us (0.958)
  the two profiles are of different devices: /device:TPU:19 before, /device:TPU:25 now
where the time goes in v3:
time: 53 us; the launch traced here: 52.9 us
  Pallas kernels  50.6 us (95%)
  local copies, waits for them, and re-layouts  2.29 us (4%)
    pallas_call x1, Pallas kernels, per_device(): pl.pallas_call(functools.partial(mixer_kernel, seq_n, chan_n, chunks, cha...  50.6 us
    unnamed x1, local copies, waits for them, and re-layouts  2.29 us

profile of v3, /device:TPU:25, one launch (start us, length us, event | category | flops | bytes accessed | tf_op | source)
XLA Modules:
  0.0 52.9 jit_solution(4948891102200118139)
XLA Ops:
  0.0 50.6 %hyena_mixers.1 = bf16[128,4096]{1,0:T(8,128)(2,1)} custom-call(bf16[128,4096]{1,0:T(8,128)(2,1)} %hid_h.1, bf16[128,4096]{1,0:T(8,128)(2,1)} %qmr_h.1, bf16[128,4096]{1,0:T(8,128)(2,1)} %kmr_h.1, bf16[128,4096]{1,0:T(8,128)(2,1)} %vmr_h.1, bf16[128,4096]{1,0:T(8,128)(2,1)} %qli_h.1, bf16[128,4096]{1,0:T(8,128)(2,1)} %kli_h.1, bf16[128,256]{1,0:T(8,128)(2,1)} %filt_h.1, ...), custom_call_target="tpu_custom_call" | custom-call | flops 2147483648 | bytes 7340032 | tf_op jit(solution)/shard_map/hyena_mixers/pallas_call | solution.py:363
  50.6 2.3 %copy.12 = bf16[128,4096]{1,0:T(8,128)(2,1)} copy(bf16[128,4096]{1,0:T(8,128)(2,1)} %hyena_mixers.1) | data formatting | bytes 2097152

commit v4 on v3

--- a/solution.py
+++ b/solution.py
@@ -10,6 +10,7 @@
 LANES = 128
 SUBS = 8
 CHUNK = LANES * SUBS
+AHEAD = 2
 f32 = jnp.float32
 bf16 = jnp.bfloat16
 
@@ -26,12 +27,12 @@
 
 def mixer_kernel(
     seq_n, chan_n, chunks, group_width,
-    hid_h, qmr_h, kmr_h, vmr_h, qli_h, kli_h, filt_h, rate_h, resid_h, gain_h,
-    out_h,
-    hid, qmr, kmr, vmr, qli, kli, filt, rate_in, resid_in, ngain,
-    prod, halo, outb, taps, upper, acc, src, rate, mgain,
+    hid_h, qmr_h, kmr_h, vmr_h, qli_h, kli_h, filt_h, rate_h, resid_h,
+    out_h, inv_h,
+    hid, qmr, kmr, vmr, qli, kli, filt, rate_in, resid_in,
+    prod, halo, inv_b, taps, upper, acc, src, rate, mgain,
     prefix, total, state_out, state_in, squares_out, squares_in,
-    in_sem, par_sem, out_sem, halo_send, halo_recv,
+    in_sem, par_sem, out_sem, inv_sem, halo_send, halo_recv,
     st_send, st_recv, sq_send, sq_recv,
 ):
     pos = lax.axis_index("seq")
@@ -56,7 +57,7 @@
     par_copies = [
         pltpu.make_async_copy(h, v, par_sem.at[i])
         for i, (h, v) in enumerate(
-            ((filt_h, filt), (rate_h, rate_in), (resid_h, resid_in), (gain_h, ngain))
+            ((filt_h, filt), (rate_h, rate_in), (resid_h, resid_in))
         )
     ]
     for k in range(chunks):
@@ -108,6 +109,12 @@
             device_id_type=pl.DeviceIdType.MESH,
         )
 
+    def start_halo(k):
+        pl.when(pos < seq_n - 1)(lambda: halo_copy(k).start())
+
+    def halo_sent(k):
+        pl.when(pos < seq_n - 1)(lambda: halo_copy(k).wait_send())
+
     @pl.when(pos == 0)
     def _():
         halo[...] = jnp.zeros_like(halo)
@@ -119,9 +126,8 @@
         if k == 0:
             pl.semaphore_wait(barrier, 2 + sum(radices) - rounds + chan_n - 1)
 
-        @pl.when(pos < seq_n - 1)
-        def _():
-            halo_copy(k).start()
+        if k < AHEAD:
+            start_halo(k)
 
     for c in par_copies:
         c.wait()
@@ -273,6 +279,9 @@
 
             takes(r, e, take)
 
+    def out_copy(k):
+        return pltpu.make_async_copy(acc.at[k], out_h.at[:, cols(k)], out_sem.at[k])
+
     def finish_chunk(k):
         decay = [jnp.exp(-chunk_mode(rate, k, n)) for n in range(modes)]
         start = tuple(
@@ -301,10 +310,14 @@
             return carry
 
         lax.fori_loop(0, SUBS, block, 0)
+        out_copy(k).start()
 
     squares_out[...] = jnp.zeros_like(squares_out)
     for turn in range(chunks + rounds):
         if turn < chunks:
+            halo_sent(turn)
+            if turn + AHEAD < chunks:
+                start_halo(turn + AHEAD)
             medium_and_states(turn)
             send_state(0, turn)
         for k in range(chunks):
@@ -325,24 +338,23 @@
         sums = sums + squares_in[d - 1]
     width = chunks * CHUNK * chan_n
     inverse = lax.rsqrt(jnp.sum(sums, 1, keepdims=True) / width + 1e-06)
+    inv_b[...] = jnp.broadcast_to(inverse, inv_b.shape)
+    inv_copy = pltpu.make_async_copy(inv_b, inv_h, inv_sem)
+    inv_copy.start()
+    inv_copy.wait()
 
     for k in range(chunks):
-        outb[k] = (acc[k] * inverse * ngain[:, cols(k)]).astype(bf16)
-        pltpu.make_async_copy(outb.at[k], out_h.at[:, cols(k)], out_sem.at[k]).start()
-
-    for k in range(chunks):
-        pltpu.make_async_copy(outb.at[k], out_h.at[:, cols(k)], out_sem.at[k]).wait()
-
-        @pl.when(pos < seq_n - 1)
-        def _():
-            halo_copy(k).wait_send()
-
+        out_copy(k).wait()
         for r in range(rounds):
             for e in range(1, radices[r]):
                 sends(r, e, lambda: state_copy(r, e, k).wait_send())
 
     for d in range(1, chan_n):
         squares_copy(d).wait_send()
+
+
+def norm_kernel(combined, inverse, gain, out):
+    out[...] = (combined[...] * inverse[:, :1] * gain[...]).astype(bf16)
 
 
 def per_device(
@@ -360,18 +372,21 @@
     assert seq_n & (seq_n - 1) == 0 and tokens == mr_filter.shape[0] == LANES
     big = pltpu.VMEM((chunks, tokens, CHUNK), bf16)
     dma = pltpu.SemaphoreType.DMA
-    return pl.pallas_call(
+    combined, inverse = pl.pallas_call(
         functools.partial(mixer_kernel, seq_n, chan_n, chunks, channels // groups),
-        out_shape=jax.ShapeDtypeStruct((tokens, channels), bf16),
-        in_specs=[pl.BlockSpec(memory_space=pl.ANY)] * 10,
-        out_specs=pl.BlockSpec(memory_space=pl.ANY),
+        out_shape=(
+            jax.ShapeDtypeStruct((tokens, channels), f32),
+            jax.ShapeDtypeStruct((tokens, LANES), f32),
+        ),
+        in_specs=[pl.BlockSpec(memory_space=pl.ANY)] * 9,
+        out_specs=(pl.BlockSpec(memory_space=pl.ANY),) * 2,
         scratch_shapes=[
             big, big, big, big, big, big,
             pltpu.VMEM(mr_filter.shape, bf16),
             pltpu.VMEM(li_rate.shape, f32),
             pltpu.VMEM(li_residue.shape, f32),
-            pltpu.VMEM((1, channels), f32),
-            big, big, big,
+            big, big,
+            pltpu.VMEM((tokens, LANES), f32),
             pltpu.VMEM((groups, tokens), f32),
             pltpu.VMEM((channels // LANES, tokens, tokens * LANES * groups // channels), bf16),
             pltpu.VMEM((chunks, tokens, CHUNK), f32),
@@ -385,8 +400,9 @@
             pltpu.VMEM((tokens, LANES), f32),
             pltpu.VMEM((max(chan_n - 1, 1), tokens, LANES), f32),
             dma((6, chunks)),
-            dma((4,)),
+            dma((3,)),
             dma((chunks,)),
+            dma,
             dma((chunks,)),
             dma((chunks,)),
             dma((rounds, most, chunks)),
@@ -405,8 +421,21 @@
         name="hyena_mixers",
     )(
         hidden_in, query_mr, key_mr, value_mr, query_li, key_li,
-        mr_filter, li_rate, li_residue, norm_gain.reshape(1, channels),
+        mr_filter, li_rate, li_residue,
     )
+    block = pl.BlockSpec((tokens, CHUNK), lambda i: (0, i))
+    return pl.pallas_call(
+        norm_kernel,
+        grid=(chunks,),
+        out_shape=jax.ShapeDtypeStruct((tokens, channels), bf16),
+        in_specs=[
+            block,
+            pl.BlockSpec((tokens, LANES), lambda i: (0, 0)),
+            pl.BlockSpec((1, CHUNK), lambda i: (0, i)),
+        ],
+        out_specs=block,
+        name="rms_scale",
+    )(combined, inverse, norm_gain.reshape(1, channels))
 
 
 def solution(mesh):

time: 53 us -> 52.5 us (level)
  local copies, waits for them, and re-layouts: 2.29 us -> 0 us
  Pallas kernels: 50.6 us -> 52.3 us
    pallas_call x0 -> x1, Pallas kernels: none -> 3.78 us  [per_device(): pl.pallas_call(norm_kernel, grid=(chunks,), out_shape=jax.ShapeDtypeStruc...]
    unnamed x1 -> x0, local copies, waits for them, and re-layouts: 2.29 us -> none
    pallas_call x1, Pallas kernels: 50.6 us -> 48.6 us  [per_device(): pl.pallas_call(functools.partial(mixer_kernel, seq_n, chan_n, chunks, cha...]
where the time goes in v4:
time: 52.5 us; the launch traced here: 52.4 us
  Pallas kernels  52.3 us (100%)
    pallas_call x1, Pallas kernels, per_device(): pl.pallas_call(functools.partial(mixer_kernel, seq_n, chan_n, chunks, cha...  48.6 us
    pallas_call x1, Pallas kernels, per_device(): pl.pallas_call(norm_kernel, grid=(chunks,), out_shape=jax.ShapeDtypeStruc...  3.78 us

profile of v4, /device:TPU:25, one launch (start us, length us, event | category | flops | bytes accessed | tf_op | source)
XLA Modules:
  0.0 52.4 jit_solution(14885835517735379431)
XLA Ops:
  0.0 48.6 %hyena_mixers.1 = (f32[128,4096]{1,0:T(8,128)}, f32[128,128]{1,0:T(8,128)}) custom-call(bf16[128,4096]{1,0:T(8,128)(2,1)} %hid_h.1, bf16[128,4096]{1,0:T(8,128)(2,1)} %qmr_h.1, bf16[128,4096]{1,0:T(8,128)(2,1)} %kmr_h.1, bf16[128,4096]{1,0:T(8,128)(2,1)} %vmr_h.1, bf16[128,4096]{1,0:T(8,128)(2,1)} %qli_h.1, bf16[128,4096]{1,0:T(8,128)(2,1)} %kli_h.1, ...), custom_call_target="tpu_custom_call" | custom-call | flops 2147483648 | bytes 7340032 | tf_op jit(solution)/shard_map/hyena_mixers/pallas_call | solution.py:375
  48.6 3.8 %rms_scale.1 = bf16[128,4096]{1,0:T(8,128)(2,1)} custom-call(f32[128,4096]{1,0:T(8,128)} %get-tuple-element.7.combined, f32[128,128]{1,0:T(8,128)} %get-tuple-element.8.inverse, f32[1,4096]{1,0:T(1,128)} %bitcast.1), custom_call_target="tpu_custom_call" | custom-call | tf_op jit(solution)/shard_map/rms_scale/pallas_call | solution.py:427

commit v5 on v3

--- a/solution.py
+++ b/solution.py
@@ -10,6 +10,8 @@
 LANES = 128
 SUBS = 8
 CHUNK = LANES * SUBS
+AHEAD = 2
+PAIR = 16
 f32 = jnp.float32
 bf16 = jnp.bfloat16
 
@@ -29,7 +31,7 @@
     hid_h, qmr_h, kmr_h, vmr_h, qli_h, kli_h, filt_h, rate_h, resid_h, gain_h,
     out_h,
     hid, qmr, kmr, vmr, qli, kli, filt, rate_in, resid_in, ngain,
-    prod, halo, outb, taps, upper, acc, src, rate, mgain,
+    spill, halo, outb, taps, acc, src, rate, mgain,
     prefix, total, state_out, state_in, squares_out, squares_in,
     in_sem, par_sem, out_sem, halo_send, halo_recv,
     st_send, st_recv, sq_send, sq_recv,
@@ -39,6 +41,7 @@
     tokens = hid.shape[1]
     modes = rate_in.shape[0]
     slab = modes * SUBS
+    pitch = tokens + SUBS
     radices, spans = stages(seq_n)
     rounds = len(radices)
     per_block = LANES // group_width
@@ -59,10 +62,11 @@
             ((filt_h, filt), (rate_h, rate_in), (resid_h, resid_in), (gain_h, ngain))
         )
     ]
+    par_copies[0].start()
     for k in range(chunks):
         in_copy(0, k).start()
         in_copy(1, k).start()
-    for c in par_copies:
+    for c in par_copies[1:]:
         c.start()
     for a in range(2, 6):
         for k in range(chunks):
@@ -88,7 +92,7 @@
 
     def halo_copy(k):
         return pltpu.make_async_remote_copy(
-            src_ref=prod.at[k], dst_ref=halo.at[k],
+            src_ref=spill.at[k], dst_ref=halo.at[k],
             send_sem=halo_send.at[k], recv_sem=halo_recv.at[k],
             device_id={"seq": nxt}, device_id_type=pl.DeviceIdType.MESH,
         )
@@ -108,20 +112,15 @@
             device_id_type=pl.DeviceIdType.MESH,
         )
 
+    def start_halo(k):
+        pl.when(pos < seq_n - 1)(lambda: halo_copy(k).start())
+
+    def halo_sent(k):
+        pl.when(pos < seq_n - 1)(lambda: halo_copy(k).wait_send())
+
     @pl.when(pos == 0)
     def _():
         halo[...] = jnp.zeros_like(halo)
-
-    for k in range(chunks):
-        in_copy(0, k).wait()
-        in_copy(1, k).wait()
-        prod[k] = (kmr[k].astype(f32) * vmr[k].astype(f32)).astype(bf16)
-        if k == 0:
-            pl.semaphore_wait(barrier, 2 + sum(radices) - rounds + chan_n - 1)
-
-        @pl.when(pos < seq_n - 1)
-        def _():
-            halo_copy(k).start()
 
     for c in par_copies:
         c.wait()
@@ -147,42 +146,48 @@
             rate[rows, :] = r
             mgain[rows, :] = resid_in[:, lanes] * jnp.sqrt(grown)
 
-    def spread(x):
-        lane = lax.broadcasted_iota(jnp.int32, x.shape, 1)
-        wide = x.astype(f32)
-        return jnp.concatenate(
-            [
-                jnp.where(lane // group_width == g, wide, 0.0).astype(bf16)
-                for g in range(per_block)
-            ],
-            0,
-        )
-
-    row_i = lax.broadcasted_iota(jnp.int32, (tokens, LANES), 0)
-    lane_i = lax.broadcasted_iota(jnp.int32, (tokens, LANES), 1)
-    lower_mask = lane_i <= row_i
+    group_of_lane = lax.broadcasted_iota(jnp.int32, (tokens, LANES), 1) // group_width
+    member_lanes = [jnp.where(group_of_lane == g, 1.0, 0.0).astype(bf16) for g in range(per_block)]
+    lags = lax.broadcasted_iota(jnp.int32, (tokens, LANES), 0) - lax.broadcasted_iota(
+        jnp.int32, (tokens, LANES), 1
+    )
+    lower = jnp.where(lags >= 0, 1.0, 0.0).astype(bf16)
+    higher = jnp.where(lags >= 0, 0.0, 1.0).astype(bf16)
 
     for k in range(chunks):
+        in_copy(0, k).wait()
+        in_copy(1, k).wait()
 
         def local_block(b, carry):
             j = k * SUBS + b
             lanes = pl.ds(pl.multiple_of(b * LANES, LANES), LANES)
+            product = (kmr[k, :, lanes].astype(f32) * vmr[k, :, lanes].astype(f32)).astype(bf16)
             rows = taps[pl.ds(pl.multiple_of(j * per_block, per_block), per_block), :]
-            lows, ups = [], []
+            own, over = [], []
             for g in range(per_block):
-                ring = pltpu.roll(
-                    jnp.broadcast_to(rows[g : g + 1, :], (tokens, LANES)),
+                first = pltpu.roll(
+                    jnp.broadcast_to(rows[g : g + 1, :], (PAIR, LANES)),
                     0, 1, stride=1, stride_axis=0,
+                ).astype(bf16)
+                ring = jnp.concatenate(
+                    [first] + [pltpu.roll(first, i, 1) for i in range(PAIR, tokens, PAIR)], 0
                 )
-                lows.append(jnp.where(lower_mask, ring, 0.0).astype(bf16))
-                ups.append(jnp.where(lower_mask, 0.0, ring).astype(bf16))
-            upper[j] = jnp.concatenate(ups, 1)
-            acc[k, :, lanes] = jnp.dot(
-                jnp.concatenate(lows, 1), spread(prod[k, :, lanes]), preferred_element_type=f32
+                own.append(ring * lower)
+                over.append(ring * higher)
+            result = jnp.dot(
+                jnp.concatenate([jnp.concatenate(own, 1), jnp.concatenate(over, 1)], 0),
+                jnp.concatenate([product * m for m in member_lanes], 0),
+                preferred_element_type=f32,
             )
+            acc[k, :, lanes] = result[:tokens]
+            spill[k, :, lanes] = result[tokens:].astype(bf16)
             return carry
 
         lax.fori_loop(0, SUBS, local_block, 0)
+        if k == 0:
+            pl.semaphore_wait(barrier, 2 + sum(radices) - rounds + chan_n - 1)
+        if k < AHEAD:
+            start_halo(k)
 
     def chunk_rate(k):
         return rate[pl.ds(k * slab, slab), :]
@@ -201,11 +206,9 @@
         def block(b, carry):
             j = k * SUBS + b
             lanes = pl.ds(pl.multiple_of(b * LANES, LANES), LANES)
-            conv = acc[k, :, lanes] + jnp.dot(
-                upper[j], spread(halo[k, :, lanes]), preferred_element_type=f32
-            )
+            conv = acc[k, :, lanes] + halo[k, :, lanes].astype(f32)
             out_mr = (qmr[k, :, lanes].astype(f32) * conv).astype(bf16).astype(f32)
-            src[pl.ds(pl.multiple_of(j * tokens, tokens), tokens), :] = (
+            src[pl.ds(pl.multiple_of(j * pitch, SUBS), tokens), :] = (
                 kli[k, :, lanes].astype(f32) * out_mr
             )
             acc[k, :, lanes] = hid[k, :, lanes].astype(f32) + out_mr
@@ -217,7 +220,7 @@
         gain = [chunk_mode(mgain, k, n) for n in range(modes)]
 
         def step(t, states):
-            at = pl.ds(k * SUBS * tokens + t, SUBS, stride=tokens)
+            at = pl.ds(k * SUBS * pitch + t, SUBS, stride=pitch)
             x = src[at, :]
             states = tuple(decay[n] * states[n] + x for n in range(modes))
             parts = [gain[n] * states[n] for n in range(modes)]
@@ -280,7 +283,7 @@
         )
 
         def step(t, waves):
-            at = pl.ds(k * SUBS * tokens + t, SUBS, stride=tokens)
+            at = pl.ds(k * SUBS * pitch + t, SUBS, stride=pitch)
             waves = tuple(decay[n] * waves[n] for n in range(modes))
             parts = list(waves)
             while len(parts) > 1:
@@ -294,7 +297,7 @@
         def block(b, carry):
             j = k * SUBS + b
             lanes = pl.ds(pl.multiple_of(b * LANES, LANES), LANES)
-            conv = src[pl.ds(pl.multiple_of(j * tokens, tokens), tokens), :]
+            conv = src[pl.ds(pl.multiple_of(j * pitch, SUBS), tokens), :]
             combined = acc[k, :, lanes] + qli[k, :, lanes].astype(f32) * conv
             acc[k, :, lanes] = combined
             squares_out[...] += combined * combined
@@ -305,6 +308,9 @@
     squares_out[...] = jnp.zeros_like(squares_out)
     for turn in range(chunks + rounds):
         if turn < chunks:
+            halo_sent(turn)
+            if turn + AHEAD < chunks:
+                start_halo(turn + AHEAD)
             medium_and_states(turn)
             send_state(0, turn)
         for k in range(chunks):
@@ -332,10 +338,6 @@
 
     for k in range(chunks):
         pltpu.make_async_copy(outb.at[k], out_h.at[:, cols(k)], out_sem.at[k]).wait()
-
-        @pl.when(pos < seq_n - 1)
-        def _():
-            halo_copy(k).wait_send()
 
         for r in range(rounds):
             for e in range(1, radices[r]):
@@ -373,9 +375,8 @@
             pltpu.VMEM((1, channels), f32),
             big, big, big,
             pltpu.VMEM((groups, tokens), f32),
-            pltpu.VMEM((channels // LANES, tokens, tokens * LANES * groups // channels), bf16),
             pltpu.VMEM((chunks, tokens, CHUNK), f32),
-            pltpu.VMEM((channels // LANES * tokens, LANES), f32),
+            pltpu.VMEM((channels // LANES * (tokens + SUBS), LANES), f32),
             pltpu.VMEM((chunks * slab, LANES), f32),
             pltpu.VMEM((chunks * slab, LANES), f32),
             pltpu.VMEM((chunks, slab, LANES), f32),

time: 53 us -> 51.8 us (0.977)
  Pallas kernels: 50.6 us -> 49.3 us
    pallas_call x1, Pallas kernels: 50.6 us -> 49.3 us  [per_device(): pl.pallas_call(functools.partial(mixer_kernel, seq_n, chan_n, chunks, cha...]
where the time goes in v5:
time: 51.8 us; the launch traced here: 51.6 us
  Pallas kernels  49.3 us (95%)
  local copies, waits for them, and re-layouts  2.29 us (4%)
    pallas_call x1, Pallas kernels, per_device(): pl.pallas_call(functools.partial(mixer_kernel, seq_n, chan_n, chunks, cha...  49.3 us
    unnamed x1, local copies, waits for them, and re-layouts  2.29 us

profile of v5, /device:TPU:25, one launch (start us, length us, event | category | flops | bytes accessed | tf_op | source)
XLA Modules:
  0.0 51.6 jit_solution(13163226449266644481)
XLA Ops:
  0.0 49.3 %hyena_mixers.1 = bf16[128,4096]{1,0:T(8,128)(2,1)} custom-call(bf16[128,4096]{1,0:T(8,128)(2,1)} %hid_h.1, bf16[128,4096]{1,0:T(8,128)(2,1)} %qmr_h.1, bf16[128,4096]{1,0:T(8,128)(2,1)} %kmr_h.1, bf16[128,4096]{1,0:T(8,128)(2,1)} %vmr_h.1, bf16[128,4096]{1,0:T(8,128)(2,1)} %qli_h.1, bf16[128,4096]{1,0:T(8,128)(2,1)} %kli_h.1, bf16[128,256]{1,0:T(8,128)(2,1)} %filt_h.1, ...), custom_call_target="tpu_custom_call" | custom-call | flops 2147483648 | bytes 7340032 | tf_op jit(solution)/shard_map/hyena_mixers/pallas_call | solution.py:365
  49.3 2.3 %copy.12 = bf16[128,4096]{1,0:T(8,128)(2,1)} copy(bf16[128,4096]{1,0:T(8,128)(2,1)} %hyena_mixers.1) | data formatting | bytes 2097152

commit v6 on v5

--- a/solution.py
+++ b/solution.py
@@ -31,7 +31,7 @@
     hid_h, qmr_h, kmr_h, vmr_h, qli_h, kli_h, filt_h, rate_h, resid_h, gain_h,
     out_h,
     hid, qmr, kmr, vmr, qli, kli, filt, rate_in, resid_in, ngain,
-    spill, halo, outb, taps, acc, src, rate, mgain,
+    spill, halo, outb, taps, upper, acc, src, rate, mgain,
     prefix, total, state_out, state_in, squares_out, squares_in,
     in_sem, par_sem, out_sem, halo_send, halo_recv,
     st_send, st_recv, sq_send, sq_recv,
@@ -122,6 +122,11 @@
     def _():
         halo[...] = jnp.zeros_like(halo)
 
+    in_copy(0, 0).wait()
+    in_copy(1, 0).wait()
+    spill[0] = (kmr[0].astype(f32) * vmr[0].astype(f32)).astype(bf16)
+    pl.semaphore_wait(barrier, 2 + sum(radices) - rounds + chan_n - 1)
+    start_halo(0)
     for c in par_copies:
         c.wait()
 
@@ -132,22 +137,12 @@
         filt[...], wrap, (((0,), (0,)), ((), ())), preferred_element_type=f32
     )
 
-    for k in range(chunks):
-        for b in range(SUBS):
-            lanes = pl.ds(k * CHUNK + b * LANES, LANES)
-            r = rate_in[:, lanes]
-            x = 2.0 * r
-            series = x * (
-                1.0 - x * (1 / 2) * (1.0 - x * (1 / 3) * (1.0 - x * (1 / 4) * (
-                    1.0 - x * (1 / 5) * (1.0 - x * (1 / 6) * (1.0 - x * (1 / 7))))))
-            )
-            grown = jnp.where(x < 0.1, series, 1.0 - jnp.exp(-x))
-            rows = pl.ds(k * slab + b, modes, stride=SUBS)
-            rate[rows, :] = r
-            mgain[rows, :] = resid_in[:, lanes] * jnp.sqrt(grown)
-
     group_of_lane = lax.broadcasted_iota(jnp.int32, (tokens, LANES), 1) // group_width
     member_lanes = [jnp.where(group_of_lane == g, 1.0, 0.0).astype(bf16) for g in range(per_block)]
+
+    def spread(x):
+        return jnp.concatenate([x * m for m in member_lanes], 0)
+
     lags = lax.broadcasted_iota(jnp.int32, (tokens, LANES), 0) - lax.broadcasted_iota(
         jnp.int32, (tokens, LANES), 1
     )
@@ -155,8 +150,9 @@
     higher = jnp.where(lags >= 0, 0.0, 1.0).astype(bf16)
 
     for k in range(chunks):
-        in_copy(0, k).wait()
-        in_copy(1, k).wait()
+        if k > 0:
+            in_copy(0, k).wait()
+            in_copy(1, k).wait()
 
         def local_block(b, carry):
             j = k * SUBS + b
@@ -174,20 +170,35 @@
                 )
                 own.append(ring * lower)
                 over.append(ring * higher)
-            result = jnp.dot(
-                jnp.concatenate([jnp.concatenate(own, 1), jnp.concatenate(over, 1)], 0),
-                jnp.concatenate([product * m for m in member_lanes], 0),
-                preferred_element_type=f32,
+            own, over = jnp.concatenate(own, 1), jnp.concatenate(over, 1)
+            if k == 0:
+                upper[b] = over
+                acc[k, :, lanes] = jnp.dot(own, spread(product), preferred_element_type=f32)
+            else:
+                result = jnp.dot(
+                    jnp.concatenate([own, over], 0), spread(product), preferred_element_type=f32
+                )
+                acc[k, :, lanes] = result[:tokens]
+                spill[k, :, lanes] = result[tokens:].astype(bf16)
+            return carry
+
+        lax.fori_loop(0, SUBS, local_block, 0)
+        if 0 < k < AHEAD:
+            start_halo(k)
+
+    for k in range(chunks):
+        for b in range(SUBS):
+            lanes = pl.ds(k * CHUNK + b * LANES, LANES)
+            r = rate_in[:, lanes]
+            x = 2.0 * r
+            series = x * (
+                1.0 - x * (1 / 2) * (1.0 - x * (1 / 3) * (1.0 - x * (1 / 4) * (
+                    1.0 - x * (1 / 5) * (1.0 - x * (1 / 6) * (1.0 - x * (1 / 7))))))
             )
-            acc[k, :, lanes] = result[:tokens]
-            spill[k, :, lanes] = result[tokens:].astype(bf16)
-            return carry
-
-        lax.fori_loop(0, SUBS, local_block, 0)
-        if k == 0:
-            pl.semaphore_wait(barrier, 2 + sum(radices) - rounds + chan_n - 1)
-        if k < AHEAD:
-            start_halo(k)
+            grown = jnp.where(x < 0.1, series, 1.0 - jnp.exp(-x))
+            rows = pl.ds(k * slab + b, modes, stride=SUBS)
+            rate[rows, :] = r
+            mgain[rows, :] = resid_in[:, lanes] * jnp.sqrt(grown)
 
     def chunk_rate(k):
         return rate[pl.ds(k * slab, slab), :]
@@ -206,7 +217,13 @@
         def block(b, carry):
             j = k * SUBS + b
             lanes = pl.ds(pl.multiple_of(b * LANES, LANES), LANES)
-            conv = acc[k, :, lanes] + halo[k, :, lanes].astype(f32)
+            if k == 0:
+                earlier = jnp.dot(
+                    upper[b], spread(halo[k, :, lanes]), preferred_element_type=f32
+                )
+            else:
+                earlier = halo[k, :, lanes].astype(f32)
+            conv = acc[k, :, lanes] + earlier
             out_mr = (qmr[k, :, lanes].astype(f32) * conv).astype(bf16).astype(f32)
             src[pl.ds(pl.multiple_of(j * pitch, SUBS), tokens), :] = (
                 kli[k, :, lanes].astype(f32) * out_mr
@@ -218,6 +235,10 @@
 
         decay = [jnp.exp(-chunk_mode(rate, k, n)) for n in range(modes)]
         gain = [chunk_mode(mgain, k, n) for n in range(modes)]
+
+        def end_step(t, states):
+            x = src[pl.ds(k * SUBS * pitch + t, SUBS, stride=pitch), :]
+            return tuple(decay[n] * states[n] + x for n in range(modes))
 
         def step(t, states):
             at = pl.ds(k * SUBS * pitch + t, SUBS, stride=pitch)
@@ -230,10 +251,16 @@
             return states
 
         zero = jnp.zeros((SUBS, LANES), f32)
-        states = lax.fori_loop(0, tokens, step, (zero,) * modes, unroll=16)
+        last = k == chunks - 1
+        states = lax.fori_loop(
+            0, tokens, end_step if last else step, (zero,) * modes, unroll=16
+        )
         for n in range(modes):
             total[k, pl.ds(n * SUBS, SUBS), :] = states[n]
         prefix[k] = jnp.zeros((slab, LANES), f32)
+        send_state(0, k)
+        if last:
+            lax.fori_loop(0, tokens, step, (zero,) * modes, unroll=16)
 
     def sends(r, e, act):
         if r < rounds - 1:
@@ -312,7 +339,6 @@
             if turn + AHEAD < chunks:
                 start_halo(turn + AHEAD)
             medium_and_states(turn)
-            send_state(0, turn)
         for k in range(chunks):
             r = turn - k - 1
             if 0 <= r < rounds:
@@ -375,6 +401,7 @@
             pltpu.VMEM((1, channels), f32),
             big, big, big,
             pltpu.VMEM((groups, tokens), f32),
+            pltpu.VMEM((SUBS, tokens, tokens * LANES * groups // channels), bf16),
             pltpu.VMEM((chunks, tokens, CHUNK), f32),
             pltpu.VMEM((channels // LANES * (tokens + SUBS), LANES), f32),
             pltpu.VMEM((chunks * slab, LANES), f32),

time: 51.8 us -> 51.9 us (level)
  no operation moved by 1% of the time
where the time goes in v6:
time: 51.9 us; the launch traced here: 51.4 us
  Pallas kernels  49.1 us (95%)
  local copies, waits for them, and re-layouts  2.29 us (4%)
    pallas_call x1, Pallas kernels, per_device(): pl.pallas_call(functools.partial(mixer_kernel, seq_n, chan_n, chunks, cha...  49.1 us
    unnamed x1, local copies, waits for them, and re-layouts  2.29 us

profile of v6, /device:TPU:25, one launch (start us, length us, event | category | flops | bytes accessed | tf_op | source)
XLA Modules:
  0.0 51.4 jit_solution(11213477428483010827)
XLA Ops:
  0.0 49.1 %hyena_mixers.1 = bf16[128,4096]{1,0:T(8,128)(2,1)} custom-call(bf16[128,4096]{1,0:T(8,128)(2,1)} %hid_h.1, bf16[128,4096]{1,0:T(8,128)(2,1)} %qmr_h.1, bf16[128,4096]{1,0:T(8,128)(2,1)} %kmr_h.1, bf16[128,4096]{1,0:T(8,128)(2,1)} %vmr_h.1, bf16[128,4096]{1,0:T(8,128)(2,1)} %qli_h.1, bf16[128,4096]{1,0:T(8,128)(2,1)} %kli_h.1, bf16[128,256]{1,0:T(8,128)(2,1)} %filt_h.1, ...), custom_call_target="tpu_custom_call" | custom-call | flops 2147483648 | bytes 7340032 | tf_op jit(solution)/shard_map/hyena_mixers/pallas_call | solution.py:391
  49.1 2.3 %copy.12 = bf16[128,4096]{1,0:T(8,128)(2,1)} copy(bf16[128,4096]{1,0:T(8,128)(2,1)} %hyena_mixers.1) | data formatting | bytes 2097152

commit v7 on v6

--- a/solution.py
+++ b/solution.py
@@ -12,6 +12,7 @@
 CHUNK = LANES * SUBS
 AHEAD = 2
 PAIR = 16
+GROUP = 8
 f32 = jnp.float32
 bf16 = jnp.bfloat16
 
@@ -31,7 +32,7 @@
     hid_h, qmr_h, kmr_h, vmr_h, qli_h, kli_h, filt_h, rate_h, resid_h, gain_h,
     out_h,
     hid, qmr, kmr, vmr, qli, kli, filt, rate_in, resid_in, ngain,
-    spill, halo, outb, taps, upper, acc, src, rate, mgain,
+    spill, halo, outb, taps, upper, acc, src, own_li, rate, fade, mgain,
     prefix, total, state_out, state_in, squares_out, squares_in,
     in_sem, par_sem, out_sem, halo_send, halo_recv,
     st_send, st_recv, sq_send, sq_recv,
@@ -198,6 +199,7 @@
             grown = jnp.where(x < 0.1, series, 1.0 - jnp.exp(-x))
             rows = pl.ds(k * slab + b, modes, stride=SUBS)
             rate[rows, :] = r
+            fade[rows, :] = jnp.exp(-r)
             mgain[rows, :] = resid_in[:, lanes] * jnp.sqrt(grown)
 
     def chunk_rate(k):
@@ -205,6 +207,9 @@
 
     def chunk_mode(ref, k, n):
         return ref[pl.ds(k * slab + n * SUBS, SUBS), :]
+
+    def at_token(k, i, u):
+        return pl.ds(k * SUBS * pitch + i * GROUP + u, SUBS, stride=pitch)
 
     def medium_and_states(k):
         @pl.when(pos > 0)
@@ -233,34 +238,41 @@
 
         lax.fori_loop(0, SUBS, block, 0)
 
-        decay = [jnp.exp(-chunk_mode(rate, k, n)) for n in range(modes)]
-        gain = [chunk_mode(mgain, k, n) for n in range(modes)]
-
-        def end_step(t, states):
-            x = src[pl.ds(k * SUBS * pitch + t, SUBS, stride=pitch), :]
-            return tuple(decay[n] * states[n] + x for n in range(modes))
-
-        def step(t, states):
-            at = pl.ds(k * SUBS * pitch + t, SUBS, stride=pitch)
-            x = src[at, :]
-            states = tuple(decay[n] * states[n] + x for n in range(modes))
-            parts = [gain[n] * states[n] for n in range(modes)]
-            while len(parts) > 1:
-                parts = [a + b for a, b in zip(parts[::2], parts[1::2])]
-            src[at, :] = parts[0]
-            return states
+        def end_step(i, states):
+            xs = [src[at_token(k, i, u), :] for u in range(GROUP)]
+            ends = []
+            for n in range(modes):
+                decay, state = chunk_mode(fade, k, n), states[n]
+                for x in xs:
+                    state = decay * state + x
+                ends.append(state)
+            return tuple(ends)
+
+        def step(i, states):
+            xs = [src[at_token(k, i, u), :] for u in range(GROUP)]
+            sums, ends = [None] * GROUP, []
+            for n in range(modes):
+                decay, gain, state = chunk_mode(fade, k, n), chunk_mode(mgain, k, n), states[n]
+                for u, x in enumerate(xs):
+                    state = decay * state + x
+                    part = gain * state
+                    sums[u] = part if n == 0 else sums[u] + part
+                ends.append(state)
+            for u in range(GROUP):
+                own_li[at_token(k, i, u), :] = sums[u]
+            return tuple(ends)
 
         zero = jnp.zeros((SUBS, LANES), f32)
         last = k == chunks - 1
         states = lax.fori_loop(
-            0, tokens, end_step if last else step, (zero,) * modes, unroll=16
+            0, tokens // GROUP, end_step if last else step, (zero,) * modes, unroll=2
         )
         for n in range(modes):
             total[k, pl.ds(n * SUBS, SUBS), :] = states[n]
         prefix[k] = jnp.zeros((slab, LANES), f32)
         send_state(0, k)
         if last:
-            lax.fori_loop(0, tokens, step, (zero,) * modes, unroll=16)
+            lax.fori_loop(0, tokens // GROUP, step, (zero,) * modes, unroll=2)
 
     def sends(r, e, act):
         if r < rounds - 1:
@@ -304,27 +316,29 @@
             takes(r, e, take)
 
     def finish_chunk(k):
-        decay = [jnp.exp(-chunk_mode(rate, k, n)) for n in range(modes)]
         start = tuple(
             chunk_mode(mgain, k, n) * prefix[k, pl.ds(n * SUBS, SUBS), :] for n in range(modes)
         )
 
-        def step(t, waves):
-            at = pl.ds(k * SUBS * pitch + t, SUBS, stride=pitch)
-            waves = tuple(decay[n] * waves[n] for n in range(modes))
-            parts = list(waves)
-            while len(parts) > 1:
-                parts = [a + b for a, b in zip(parts[::2], parts[1::2])]
-            src[at, :] = src[at, :] + parts[0]
-            return waves
-
-        lax.fori_loop(0, tokens, step, start, unroll=16)
+        def step(i, waves):
+            sums, ends = [own_li[at_token(k, i, u), :] for u in range(GROUP)], []
+            for n in range(modes):
+                decay, wave = chunk_mode(fade, k, n), waves[n]
+                for u in range(GROUP):
+                    wave = decay * wave
+                    sums[u] = sums[u] + wave
+                ends.append(wave)
+            for u in range(GROUP):
+                own_li[at_token(k, i, u), :] = sums[u]
+            return tuple(ends)
+
+        lax.fori_loop(0, tokens // GROUP, step, start, unroll=2)
         in_copy(5, k).wait()
 
         def block(b, carry):
             j = k * SUBS + b
             lanes = pl.ds(pl.multiple_of(b * LANES, LANES), LANES)
-            conv = src[pl.ds(pl.multiple_of(j * pitch, SUBS), tokens), :]
+            conv = own_li[pl.ds(pl.multiple_of(j * pitch, SUBS), tokens), :]
             combined = acc[k, :, lanes] + qli[k, :, lanes].astype(f32) * conv
             acc[k, :, lanes] = combined
             squares_out[...] += combined * combined
@@ -404,6 +418,8 @@
             pltpu.VMEM((SUBS, tokens, tokens * LANES * groups // channels), bf16),
             pltpu.VMEM((chunks, tokens, CHUNK), f32),
             pltpu.VMEM((channels // LANES * (tokens + SUBS), LANES), f32),
+            pltpu.VMEM((channels // LANES * (tokens + SUBS), LANES), f32),
+            pltpu.VMEM((chunks * slab, LANES), f32),
             pltpu.VMEM((chunks * slab, LANES), f32),
             pltpu.VMEM((chunks * slab, LANES), f32),
             pltpu.VMEM((chunks, slab, LANES), f32),

time: 51.9 us -> 51.9 us (level)
  no operation moved by 1% of the time
where the time goes in v7:
time: 51.9 us; the launch traced here: 51.6 us
  Pallas kernels  49.3 us (95%)
  local copies, waits for them, and re-layouts  2.29 us (4%)
    pallas_call x1, Pallas kernels, per_device(): pl.pallas_call(functools.partial(mixer_kernel, seq_n, chan_n, chunks, cha...  49.3 us
    unnamed x1, local copies, waits for them, and re-layouts  2.29 us

profile of v7, /device:TPU:25, one launch (start us, length us, event | category | flops | bytes accessed | tf_op | source)
XLA Modules:
  0.0 51.6 jit_solution(1647725677713444715)
XLA Ops:
  0.0 49.3 %hyena_mixers.1 = bf16[128,4096]{1,0:T(8,128)(2,1)} custom-call(bf16[128,4096]{1,0:T(8,128)(2,1)} %hid_h.1, bf16[128,4096]{1,0:T(8,128)(2,1)} %qmr_h.1, bf16[128,4096]{1,0:T(8,128)(2,1)} %kmr_h.1, bf16[128,4096]{1,0:T(8,128)(2,1)} %vmr_h.1, bf16[128,4096]{1,0:T(8,128)(2,1)} %qli_h.1, bf16[128,4096]{1,0:T(8,128)(2,1)} %kli_h.1, bf16[128,256]{1,0:T(8,128)(2,1)} %filt_h.1, ...), custom_call_target="tpu_custom_call" | custom-call | flops 2147483648 | bytes 7340032 | tf_op jit(solution)/shard_map/hyena_mixers/pallas_call | solution.py:405
  49.3 2.3 %copy.12 = bf16[128,4096]{1,0:T(8,128)(2,1)} copy(bf16[128,4096]{1,0:T(8,128)(2,1)} %hyena_mixers.1) | data formatting | bytes 2097152

commit v8 on v7

--- a/solution.py
+++ b/solution.py
@@ -10,7 +10,7 @@
 LANES = 128
 SUBS = 8
 CHUNK = LANES * SUBS
-AHEAD = 2
+AHEAD = 4
 PAIR = 16
 GROUP = 8
 f32 = jnp.float32

time: 51.9 us -> 51.2 us (0.987)
  Pallas kernels: 49.3 us -> 48.2 us
    pallas_call x1, Pallas kernels: 49.3 us -> 48.2 us  [per_device(): pl.pallas_call(functools.partial(mixer_kernel, seq_n, chan_n, chunks, cha...]
where the time goes in v8:
time: 51.2 us; the launch traced here: 50.5 us
  Pallas kernels  48.2 us (94%)
  local copies, waits for them, and re-layouts  2.29 us (4%)
    pallas_call x1, Pallas kernels, per_device(): pl.pallas_call(functools.partial(mixer_kernel, seq_n, chan_n, chunks, cha...  48.2 us
    unnamed x1, local copies, waits for them, and re-layouts  2.29 us

profile of v8, /device:TPU:25, one launch (start us, length us, event | category | flops | bytes accessed | tf_op | source)
XLA Modules:
  0.0 50.5 jit_solution(7820815628442407192)
XLA Ops:
  0.0 48.2 %hyena_mixers.1 = bf16[128,4096]{1,0:T(8,128)(2,1)} custom-call(bf16[128,4096]{1,0:T(8,128)(2,1)} %hid_h.1, bf16[128,4096]{1,0:T(8,128)(2,1)} %qmr_h.1, bf16[128,4096]{1,0:T(8,128)(2,1)} %kmr_h.1, bf16[128,4096]{1,0:T(8,128)(2,1)} %vmr_h.1, bf16[128,4096]{1,0:T(8,128)(2,1)} %qli_h.1, bf16[128,4096]{1,0:T(8,128)(2,1)} %kli_h.1, bf16[128,256]{1,0:T(8,128)(2,1)} %filt_h.1, ...), custom_call_target="tpu_custom_call" | custom-call | flops 2147483648 | bytes 7340032 | tf_op jit(solution)/shard_map/hyena_mixers/pallas_call | solution.py:405
  48.2 2.3 %copy.12 = bf16[128,4096]{1,0:T(8,128)(2,1)} copy(bf16[128,4096]{1,0:T(8,128)(2,1)} %hyena_mixers.1) | data formatting | bytes 2097152
